TPU v7x, 32 devices: a whole 2x2x4 slice. The times are simulated.
32 devices in a mesh: slab: 16 (over z, x, core), tile: 2 (over y).
Axes of the slice: x: 2, y: 2, z: 4, core: 2. Of those that a mesh axis runs over, the one named last changes fastest.
Arguments:
- position: float32 [3, 262144], P(None, ('slab', 'tile')), may hold values from 0 to 2.5
- velocity: float32 [3, 262144], P(None, ('slab', 'tile')), may hold values from -6 to 6
- particle_mass: float32 [262144], P(('slab', 'tile')), may hold values from 0.005 to 0.02
- density: float32 [262144], P(('slab', 'tile')), may hold values from 0.8 to 1.25
- deviator: float32 [6, 262144], P(None, ('slab', 'tile')), may hold values from -4 to 4
- plastic: float32 [262144], P(('slab', 'tile')), may hold values from 0.001 to 0.3
- energy: float32 [262144], P(('slab', 'tile')), may hold values from 0.05 to 1
- block_fill: int32 [2048], P(('slab', 'tile')), may hold values from 32 to 128
- pair_blocks: int32 [2, 2048], P(None, ('slab', 'tile')), may hold values from 0 to 127, as said below
- pair_count: int32 [32], P(('slab', 'tile')), may hold values from 8 to 64, as said below
- slab_send: int32 [2, 512], P(None, ('slab', 'tile')), may hold values from 0 to 63
- tile_send: int32 [2, 512], P(None, ('slab', 'tile')), may hold values from 0 to 95
Outputs:
- motion: float32 [4, 262144], P(None, ('slab', 'tile'))
- material: float32 [8, 262144], P(None, ('slab', 'tile'))
Inputs may be any that keep to these rules, and one draw needn't show every extreme that they name: `pair_blocks`: row 0 names a block of the device's own 64; row 1 any block of its table of 128: own blocks, then 16 from the lower and 16 from the upper slab neighbour, then 16 from the lower and 16 from the upper tile neighbour. A pair may repeat or name one block twice. `pair_count`: slots from the first up to this count are live, the rest are padding. Loads differ strongly between devices, and some device has all 64 slots live. `block_fill`: the live particles of a block are its first slots. `slab_send`: row 0 lists 16 own blocks for the lower, row 1 for the upper slab neighbour; repeats are allowed. `tile_send`: row 0 lists 16 blocks for the lower, row 1 for the upper tile neighbour, as indices into the extended list of own blocks and received slab blocks; repeats are allowed.
All inputs are finite; a program needn't handle non-finite values.
Results may differ from a plain program's by a relative error of at most 0.0003.
Values sent between devices are 32-bit elements; how exact they have to be, the bound alone decides.
A program may use at most 64 MiB of HBM per device.

v0:
```python
import math

import jax
import jax.numpy as jnp
from jax import lax
from jax.sharding import PartitionSpec as P

PGROUP = 16
SWEEPS = 3


SMOOTHING = 1.0
KERNEL_SCALE = -105.0 / (16.0 * math.pi)
TIME_STEP = 0.05
SHEAR_MODULUS = 1.0
BULK_MODULUS = 2.0
DENSITY_REF = 1.0
YIELD_BASE = 0.3
HARDEN_COEF = 2.0
HARDEN_EXPONENT = 0.31
RATE_COEF = 0.025
RATE_REF = 0.02
THERMAL_EXPONENT = 1.09
ENERGY_REF = 1.0
VISCOUS_ALPHA = 1.0
VISCOUS_BETA = 2.0
SOFTENING = 0.01
STRESS_FLOOR = 0.1


def extended(shard, sides, width):
    for axis, dim in sides:
        size, length = (lax.axis_size(axis), shard.shape[dim])
        up = [(i, (i + 1) % size) for i in range(size - 1)]
        down = [(j, i) for i, j in up]
        last = lax.slice_in_dim(shard, length - width, length, axis=dim)
        first = lax.slice_in_dim(shard, 0, width, axis=dim)
        before = lax.ppermute(last, axis, up)
        after = lax.ppermute(first, axis, down)
        shard = jnp.concatenate([before, shard, after], axis=dim)
    return shard


def sym_matrix(components):
    return [
        [components[0], components[3], components[5]],
        [components[3], components[1], components[4]],
        [components[5], components[4], components[2]],
    ]


def kernel_terms(first_pos, second_pos):
    deltas = [first_pos[:, k, :, None] - second_pos[:, k, None, :] for k in range(3)]
    radius_sq = deltas[0] * deltas[0] + deltas[1] * deltas[1] + deltas[2] * deltas[2]
    spread = jnp.maximum(1.0 - 0.5 * jnp.sqrt(radius_sq) / SMOOTHING, 0.0)
    factor = KERNEL_SCALE * spread * spread * spread
    return (deltas, radius_sq, [factor * one_delta for one_delta in deltas])


def gradient_terms(first_blocks, second_blocks):
    deltas, radius_sq, gradients = kernel_terms(first_blocks[:, 0:3], second_blocks[:, 0:3])
    first_volume = first_blocks[:, 7, :, None]
    second_volume = second_blocks[:, 7, None, :]
    to_first = []
    to_second = []
    for a in range(3):
        vel_diff = second_blocks[:, 3 + a, None, :] - first_blocks[:, 3 + a, :, None]
        for b in range(3):
            product = vel_diff * gradients[b]
            to_first.append(jnp.sum(product * second_volume, axis=2))
            to_second.append(jnp.sum(product * first_volume, axis=1))
    return (jnp.stack(to_first, 1), jnp.stack(to_second, 1))


def force_terms(first_blocks, second_blocks):
    deltas, radius_sq, gradients = kernel_terms(first_blocks[:, 0:3], second_blocks[:, 0:3])
    vel_diff = [
        first_blocks[:, 3 + k, :, None] - second_blocks[:, 3 + k, None, :] for k in range(3)
    ]
    approach = vel_diff[0] * deltas[0] + vel_diff[1] * deltas[1] + vel_diff[2] * deltas[2]
    closing = (
        SMOOTHING * jnp.minimum(approach, 0.0) / (radius_sq + SOFTENING * SMOOTHING * SMOOTHING)
    )
    mean_sound = 0.5 * (first_blocks[:, 14, :, None] + second_blocks[:, 14, None, :])
    mean_density = 0.5 * (first_blocks[:, 7, :, None] + second_blocks[:, 7, None, :])
    viscous = (
        -VISCOUS_ALPHA * mean_sound * closing + VISCOUS_BETA * closing * closing
    ) / mean_density
    first_stress = sym_matrix([first_blocks[:, 8 + k, :, None] for k in range(6)])
    second_stress = sym_matrix([second_blocks[:, 8 + k, None, :] for k in range(6)])
    pull_terms = []
    for a in range(3):
        summed = -viscous * gradients[a]
        for b in range(3):
            summed = summed + (first_stress[a][b] + second_stress[a][b]) * gradients[b]
        pull_terms.append(summed)
    heating = -0.5 * (
        vel_diff[0] * pull_terms[0] + vel_diff[1] * pull_terms[1] + vel_diff[2] * pull_terms[2]
    )
    first_mass = first_blocks[:, 6, :, None]
    second_mass = second_blocks[:, 6, None, :]
    to_first = [jnp.sum(second_mass * pull_term, axis=2) for pull_term in pull_terms]
    to_first.append(jnp.sum(second_mass * heating, axis=2))
    to_second = [-jnp.sum(first_mass * pull_term, axis=1) for pull_term in pull_terms]
    to_second.append(jnp.sum(first_mass * heating, axis=1))
    return (jnp.stack(to_first, 1), jnp.stack(to_second, 1))


def pair_pass(table_blocks, first_ids, second_ids, pair_live, term_fn, term_width, group_total):

    def one_group(group_index, summed):
        start_row = group_index * PGROUP
        first_rows = lax.dynamic_slice_in_dim(first_ids, start_row, PGROUP)
        second_rows = lax.dynamic_slice_in_dim(second_ids, start_row, PGROUP)
        weights = lax.dynamic_slice_in_dim(pair_live, start_row, PGROUP)
        to_first, to_second = term_fn(table_blocks[first_rows], table_blocks[second_rows])
        mirror = weights * (first_rows != second_rows).astype(jnp.float32)
        summed = summed.at[first_rows].add(to_first * weights[:, None, None])
        return summed.at[second_rows].add(to_second * mirror[:, None, None])

    zero_sums = jnp.zeros((table_blocks.shape[0], term_width, table_blocks.shape[2]), jnp.float32)
    return lax.fori_loop(0, group_total, one_group, zero_sums)


def update_material(velocity_grad, deviator, plastic, energy, density):
    gradient_rows = [[velocity_grad[3 * a + b] for b in range(3)] for a in range(3)]
    strain = [
        [0.5 * (gradient_rows[a][b] + gradient_rows[b][a]) for b in range(3)] for a in range(3)
    ]
    rotation = [
        [0.5 * (gradient_rows[a][b] - gradient_rows[b][a]) for b in range(3)] for a in range(3)
    ]
    trace_rate = strain[0][0] + strain[1][1] + strain[2][2]
    new_density = density * jnp.exp(-TIME_STEP * trace_rate)
    mean_normal = (deviator[0] + deviator[1] + deviator[2]) / 3.0
    previous = sym_matrix(
        [
            deviator[0] - mean_normal,
            deviator[1] - mean_normal,
            deviator[2] - mean_normal,
            deviator[3],
            deviator[4],
            deviator[5],
        ]
    )
    shear_rate = [
        [strain[a][b] - trace_rate / 3.0 if a == b else strain[a][b] for b in range(3)]
        for a in range(3)
    ]
    trial_stress = []
    for a in range(3):
        trial_row = []
        for b in range(3):
            rate_term = 2.0 * SHEAR_MODULUS * shear_rate[a][b]
            for k in range(3):
                rate_term = (
                    rate_term + rotation[a][k] * previous[k][b] - previous[a][k] * rotation[k][b]
                )
            trial_row.append(previous[a][b] + TIME_STEP * rate_term)
        trial_stress.append(trial_row)
    trial_parts = [
        trial_stress[0][0],
        trial_stress[1][1],
        trial_stress[2][2],
        trial_stress[0][1],
        trial_stress[1][2],
        trial_stress[2][0],
    ]
    contract = (
        trial_parts[0] * trial_parts[0]
        + trial_parts[1] * trial_parts[1]
        + trial_parts[2] * trial_parts[2]
        + 2.0
        * (
            trial_parts[3] * trial_parts[3]
            + trial_parts[4] * trial_parts[4]
            + trial_parts[5] * trial_parts[5]
        )
    )
    equivalent = jnp.sqrt(1.5 * contract)
    rate_square = shear_rate[0][0] * shear_rate[0][0]
    for a in range(3):
        for b in range(3):
            if a + b > 0:
                rate_square = rate_square + shear_rate[a][b] * shear_rate[a][b]
    rate_equiv = jnp.sqrt(2.0 / 3.0 * rate_square)
    rate_factor = 1.0 + RATE_COEF * jnp.log(jnp.maximum(rate_equiv / RATE_REF, 1.0))
    homologous = energy / (energy + ENERGY_REF)
    scale_now = rate_factor * (1.0 - homologous**THERMAL_EXPONENT)
    tangent = (
        3.0 * SHEAR_MODULUS
        + HARDEN_COEF * HARDEN_EXPONENT * plastic ** (HARDEN_EXPONENT - 1.0) * scale_now
    )
    increment = jnp.zeros_like(plastic)
    for sweep_index in range(SWEEPS):
        flow_stress = (
            YIELD_BASE + HARDEN_COEF * (plastic + increment) ** HARDEN_EXPONENT
        ) * scale_now
        increment = jnp.maximum(
            increment + (equivalent - 3.0 * SHEAR_MODULUS * increment - flow_stress) / tangent, 0.0
        )
    shrink = 1.0 - 3.0 * SHEAR_MODULUS * increment / jnp.maximum(equivalent, STRESS_FLOOR)
    new_deviator = [component * shrink for component in trial_parts]
    pressure = BULK_MODULUS * (new_density / DENSITY_REF - 1.0)
    inverse_sq = 1.0 / (new_density * new_density)
    scaled = [
        (new_deviator[k] - pressure) * inverse_sq if k < 3 else new_deviator[k] * inverse_sq
        for k in range(6)
    ]
    sound_speed = jnp.sqrt((BULK_MODULUS + 4.0 / 3.0 * SHEAR_MODULUS) / new_density)
    return (new_deviator, plastic + increment, new_density, scaled, sound_speed)


def spread_ghosts(own_blocks, slab_rows, tile_rows):
    ghost_count = slab_rows.shape[1]
    outgoing = own_blocks[slab_rows.reshape(-1)].reshape((2, ghost_count) + own_blocks.shape[1:])
    framed = extended(outgoing, (("slab", 0),), 1)
    widened = jnp.concatenate([own_blocks, framed[0], framed[3]], 0)
    outgoing = widened[tile_rows.reshape(-1)].reshape((2, ghost_count) + own_blocks.shape[1:])
    framed = extended(outgoing, (("tile", 0),), 1)
    return jnp.concatenate([widened, framed[0], framed[3]], 0)


def return_ghosts(summed, blocks_here, slab_rows, tile_rows):
    ghost_count = slab_rows.shape[1]
    inner_end = blocks_here + 2 * ghost_count
    returning = jnp.stack(
        [summed[inner_end : inner_end + ghost_count], summed[inner_end + ghost_count :]]
    )
    framed = extended(returning, (("tile", 0),), 1)
    widened = summed[:inner_end].at[tile_rows[0]].add(framed[0]).at[tile_rows[1]].add(framed[3])
    returning = jnp.stack(
        [
            widened[blocks_here : blocks_here + ghost_count],
            widened[blocks_here + ghost_count : inner_end],
        ]
    )
    framed = extended(returning, (("slab", 0),), 1)
    return widened[:blocks_here].at[slab_rows[0]].add(framed[0]).at[slab_rows[1]].add(framed[3])


def body(
    position,
    velocity,
    particle_mass,
    density,
    deviator,
    plastic,
    energy,
    block_fill,
    pair_blocks,
    pair_count,
    slab_send,
    tile_send,
):
    blocks_here = block_fill.shape[0]
    block_size = position.shape[1] // blocks_here
    slot_index = lax.broadcasted_iota(jnp.int32, (blocks_here, block_size), 1)
    alive_mask = (slot_index < block_fill[:, None]).astype(jnp.float32).reshape(-1)
    live_mass = particle_mass * alive_mask
    volume = live_mass / density

    def as_blocks(fields):
        return fields.reshape(fields.shape[0], blocks_here, block_size).transpose(1, 0, 2)

    first_ids = pair_blocks[0]
    second_ids = pair_blocks[1]
    pair_live = (jnp.arange(first_ids.shape[0], dtype=jnp.int32) < pair_count[0]).astype(
        jnp.float32
    )
    group_total = (pair_count[0] + PGROUP - 1) // PGROUP
    first_state = as_blocks(jnp.concatenate([position, velocity, live_mass[None], volume[None]], 0))
    table_one = spread_ghosts(first_state, slab_send, tile_send)
    summed = pair_pass(table_one, first_ids, second_ids, pair_live, gradient_terms, 9, group_total)
    grad_blocks = return_ghosts(summed, blocks_here, slab_send, tile_send)
    velocity_grad = grad_blocks.transpose(1, 0, 2).reshape(9, -1)
    new_deviator, new_plastic, new_density, scaled, sound_speed = update_material(
        velocity_grad, deviator, plastic, energy, density
    )
    second_state = as_blocks(
        jnp.concatenate(
            [
                position,
                velocity,
                live_mass[None],
                new_density[None],
                jnp.stack(scaled),
                sound_speed[None],
            ],
            0,
        )
    )
    table_two = spread_ghosts(second_state, slab_send, tile_send)
    summed = pair_pass(table_two, first_ids, second_ids, pair_live, force_terms, 4, group_total)
    motion_blocks = return_ghosts(summed, blocks_here, slab_send, tile_send)
    motion = motion_blocks.transpose(1, 0, 2).reshape(4, -1)
    material = jnp.concatenate([jnp.stack(new_deviator), new_plastic[None], new_density[None]], 0)
    return (motion, material)


def solution(mesh):
    placed = (
        P(None, ("slab", "tile")),
        P(None, ("slab", "tile")),
        P(("slab", "tile")),
        P(("slab", "tile")),
        P(None, ("slab", "tile")),
        P(("slab", "tile")),
        P(("slab", "tile")),
        P(("slab", "tile")),
        P(None, ("slab", "tile")),
        P(("slab", "tile")),
        P(None, ("slab", "tile")),
        P(None, ("slab", "tile")),
    )
    return jax.shard_map(
        body,
        mesh=mesh,
        in_specs=placed,
        out_specs=(P(None, ("slab", "tile")), P(None, ("slab", "tile"))),
        check_vma=False,
    )
```

profile of v0, /device:TPU:11, one launch (start us, length us, event | category | flops | bytes accessed | tf_op | source)
XLA Modules:
  0.0 276.6 jit_solution(8396836325764770594)
XLA Ops:
  23.1 39.4 %while.22 = (s32[]{:T(128)}, f32[128,9,128]{2,1,0:T(8,128)S(1)}, s32[]{:T(128)}, s32[64]{0:T(128)S(1)}, s32[64]{0:T(128)S(1)}, /*index=5*/f32[128,8,128]{2,1,0:T...) while((s32[]{:T(128)}, f32[128,9,128]{2,1,0:T(8,128)S(1)}, ...), condition=%wide.region_21.22_spmd, body=%wide.region_0.21_spmd.sunk | while | flops 17078404 | bytes 2090211 | solution.py:122
  24.5 5.7 %multiply_reduce_fusion.35 = (f32[16,128]{1,0:T(8,128)S(1)}, f32[16,128]{1,0:T(8,128)S(1)}, f32[16,128]{1,0:T(8,128)S(1)}, f32[16,128]{1,0:T(8,128)S(1)}, f32[16...) fusion(f32[16,128]{1,0:T(8,128)S(1)} %bitcast.402, ...), kind=kLoop, calls=%fused_computation.48.clone.1 | loop fusion | flops 17002496 | bytes 262144 | tf_op jit(solution)/shard_map/while/body/reduce_sum | solution.py:71
  34.3 5.7 %multiply_reduce_fusion.35 = (f32[16,128]{1,0:T(8,128)S(1)}, f32[16,128]{1,0:T(8,128)S(1)}, f32[16,128]{1,0:T(8,128)S(1)}, f32[16,128]{1,0:T(8,128)S(1)}, f32[16...) fusion(f32[16,128]{1,0:T(8,128)S(1)} %bitcast.402, ...), kind=kLoop, calls=%fused_computation.48.clone.1 | loop fusion | flops 17002496 | bytes 262144 | tf_op jit(solution)/shard_map/while/body/reduce_sum | solution.py:71
  44.1 5.7 %multiply_reduce_fusion.35 = (f32[16,128]{1,0:T(8,128)S(1)}, f32[16,128]{1,0:T(8,128)S(1)}, f32[16,128]{1,0:T(8,128)S(1)}, f32[16,128]{1,0:T(8,128)S(1)}, f32[16...) fusion(f32[16,128]{1,0:T(8,128)S(1)} %bitcast.402, ...), kind=kLoop, calls=%fused_computation.48.clone.1 | loop fusion | flops 17002496 | bytes 262144 | tf_op jit(solution)/shard_map/while/body/reduce_sum | solution.py:71
  54.0 5.7 %multiply_reduce_fusion.35 = (f32[16,128]{1,0:T(8,128)S(1)}, f32[16,128]{1,0:T(8,128)S(1)}, f32[16,128]{1,0:T(8,128)S(1)}, f32[16,128]{1,0:T(8,128)S(1)}, f32[16...) fusion(f32[16,128]{1,0:T(8,128)S(1)} %bitcast.402, ...), kind=kLoop, calls=%fused_computation.48.clone.1 | loop fusion | flops 17002496 | bytes 262144 | tf_op jit(solution)/shard_map/while/body/reduce_sum | solution.py:71
  89.5 4.7 %collective-permute-done.9 = f32[1,16,15,128]{3,2,1,0:T(8,128)S(1)} collective-permute-done((f32[1,16,15,128]{3,2,1,0:T(8,128)S(1)}, f32[1,16,15,128]{3,2,1,0:T(8,128)S(1)}, u32[]{:S(2)}, u32[]{:S(2)}) %collective-permute-start.9) | collective-permute-done | bytes 122912 | tf_op jit(solution)/shard_map/ppermute | solution.py:39
  103.5 156.1 %while.23 = (s32[]{:T(128)}, f32[128,4,128]{2,1,0:T(4,128)S(1)}, s32[]{:T(128)}, s32[64]{0:T(128)S(1)}, s32[64]{0:T(128)S(1)}, /*index=5*/f32[128,15,128]{2,1,0:...) while((s32[]{:T(128)}, f32[128,4,128]{2,1,0:T(4,128)S(1)}, ...), condition=%wide.region_37.38_spmd, body=%wide.region_26.37_spmd.sunk | while | flops 113324160 | bytes 3204323 | solution.py:122
  117.1 5.0 %multiply_reduce_fusion.40 = f32[16,128]{1,0:T(8,128)S(1)} fusion(f32[16,128]{1,0:T(8,128)S(1)} %broadcast_multiply_fusion.11, f32[16,128]{1,0:T(8,128)S(1)} %bitcast.501, f32[16,128]{1,0:T(8,128)S(1)} %bitcast.505, f32[16,128]{1,0:T(8,128)S(1)} %bitcast.420, f32[16,128]{1,0:T(8,128)S(1)} %bitcast.510, f32[16,128]{1,0:T(8,128)S(1)} %bitcast.425, ...), kind=kLoop, calls=%fused_computation.127.clone.1 | loop fusion | flops 18348032 | bytes 245760 | tf_op jit(solution)/shard_map/while/body/reduce_sum | solution.py:105
  122.4 4.2 %multiply_reduce_fusion.39 = f32[16,128]{1,0:T(8,128)S(1)} fusion(f32[16,128]{1,0:T(8,128)S(1)} %bitcast.377, f32[16,128]{1,0:T(8,128)S(1)} %bitcast.431, f32[16,128]{1,0:T(8,128)S(1)} %bitcast.521, f32[16,128]{1,0:T(8,128)S(1)} %bitcast.437, f32[16,128]{1,0:T(8,128)S(1)} %bitcast.527, f32[16,128]{1,0:T(8,128)S(1)} %bitcast.442, ...), kind=kLoop, calls=%fused_computation.134.clone.1 | loop fusion | flops 12580864 | bytes 196608 | tf_op jit(solution)/shard_map/while/body/reduce_sum | solution.py:102
  126.6 4.2 %multiply_reduce_fusion.38 = f32[16,128]{1,0:T(8,128)S(1)} fusion(f32[16,128]{1,0:T(8,128)S(1)} %bitcast.378, f32[16,128]{1,0:T(8,128)S(1)} %bitcast.421, f32[16,128]{1,0:T(8,128)S(1)} %bitcast.511, f32[16,128]{1,0:T(8,128)S(1)} %bitcast.426, f32[16,128]{1,0:T(8,128)S(1)} %bitcast.516, f32[16,128]{1,0:T(8,128)S(1)} %bitcast.438, ...), kind=kLoop, calls=%fused_computation.133.clone.1 | loop fusion | flops 12843008 | bytes 196608 | tf_op jit(solution)/shard_map/while/body/reduce_sum | solution.py:102
  130.8 4.2 %multiply_reduce_fusion.37 = f32[16,128]{1,0:T(8,128)S(1)} fusion(f32[16,128]{1,0:T(8,128)S(1)} %bitcast.379, f32[16,128]{1,0:T(8,128)S(1)} %bitcast.502, f32[16,128]{1,0:T(8,128)S(1)} %bitcast.506, f32[16,128]{1,0:T(8,128)S(1)} %bitcast.422, f32[16,128]{1,0:T(8,128)S(1)} %bitcast.512, f32[16,128]{1,0:T(8,128)S(1)} %bitcast.432, ...), kind=kLoop, calls=%fused_computation.132.clone.1 | loop fusion | flops 12843008 | bytes 196608 | tf_op jit(solution)/shard_map/while/body/reduce_sum | solution.py:102
  135.1 5.3 %multiply_reduce_fusion.36 = f32[16,128]{1,0:T(8,128)S(1)} fusion(f32[16,128]{1,0:T(8,128)S(1)} %broadcast_multiply_fusion.10, f32[16,128]{1,0:T(8,128)S(1)} %bitcast.503, f32[16,128]{1,0:T(8,128)S(1)} %bitcast.507, f32[16,128]{1,0:T(8,128)S(1)} %bitcast.423, f32[16,128]{1,0:T(8,128)S(1)} %bitcast.513, f32[16,128]{1,0:T(8,128)S(1)} %bitcast.427, ...), kind=kLoop, calls=%fused_computation.131.clone.1 | loop fusion | flops 18348032 | bytes 245760 | tf_op jit(solution)/shard_map/while/body/reduce_sum | solution.py:103
  156.1 5.0 %multiply_reduce_fusion.40 = f32[16,128]{1,0:T(8,128)S(1)} fusion(f32[16,128]{1,0:T(8,128)S(1)} %broadcast_multiply_fusion.11, f32[16,128]{1,0:T(8,128)S(1)} %bitcast.501, f32[16,128]{1,0:T(8,128)S(1)} %bitcast.505, f32[16,128]{1,0:T(8,128)S(1)} %bitcast.420, f32[16,128]{1,0:T(8,128)S(1)} %bitcast.510, f32[16,128]{1,0:T(8,128)S(1)} %bitcast.425, ...), kind=kLoop, calls=%fused_computation.127.clone.1 | loop fusion | flops 18348032 | bytes 245760 | tf_op jit(solution)/shard_map/while/body/reduce_sum | solution.py:105
  165.6 4.2 %multiply_reduce_fusion.38 = f32[16,128]{1,0:T(8,128)S(1)} fusion(f32[16,128]{1,0:T(8,128)S(1)} %bitcast.378, f32[16,128]{1,0:T(8,128)S(1)} %bitcast.421, f32[16,128]{1,0:T(8,128)S(1)} %bitcast.511, f32[16,128]{1,0:T(8,128)S(1)} %bitcast.426, f32[16,128]{1,0:T(8,128)S(1)} %bitcast.516, f32[16,128]{1,0:T(8,128)S(1)} %bitcast.438, ...), kind=kLoop, calls=%fused_computation.133.clone.1 | loop fusion | flops 12843008 | bytes 196608 | tf_op jit(solution)/shard_map/while/body/reduce_sum | solution.py:102
  169.8 4.2 %multiply_reduce_fusion.37 = f32[16,128]{1,0:T(8,128)S(1)} fusion(f32[16,128]{1,0:T(8,128)S(1)} %bitcast.379, f32[16,128]{1,0:T(8,128)S(1)} %bitcast.502, f32[16,128]{1,0:T(8,128)S(1)} %bitcast.506, f32[16,128]{1,0:T(8,128)S(1)} %bitcast.422, f32[16,128]{1,0:T(8,128)S(1)} %bitcast.512, f32[16,128]{1,0:T(8,128)S(1)} %bitcast.432, ...), kind=kLoop, calls=%fused_computation.132.clone.1 | loop fusion | flops 12843008 | bytes 196608 | tf_op jit(solution)/shard_map/while/body/reduce_sum | solution.py:102
  174.1 5.3 %multiply_reduce_fusion.36 = f32[16,128]{1,0:T(8,128)S(1)} fusion(f32[16,128]{1,0:T(8,128)S(1)} %broadcast_multiply_fusion.10, f32[16,128]{1,0:T(8,128)S(1)} %bitcast.503, f32[16,128]{1,0:T(8,128)S(1)} %bitcast.507, f32[16,128]{1,0:T(8,128)S(1)} %bitcast.423, f32[16,128]{1,0:T(8,128)S(1)} %bitcast.513, f32[16,128]{1,0:T(8,128)S(1)} %bitcast.427, ...), kind=kLoop, calls=%fused_computation.131.clone.1 | loop fusion | flops 18348032 | bytes 245760 | tf_op jit(solution)/shard_map/while/body/reduce_sum | solution.py:103
  195.1 5.0 %multiply_reduce_fusion.40 = f32[16,128]{1,0:T(8,128)S(1)} fusion(f32[16,128]{1,0:T(8,128)S(1)} %broadcast_multiply_fusion.11, f32[16,128]{1,0:T(8,128)S(1)} %bitcast.501, f32[16,128]{1,0:T(8,128)S(1)} %bitcast.505, f32[16,128]{1,0:T(8,128)S(1)} %bitcast.420, f32[16,128]{1,0:T(8,128)S(1)} %bitcast.510, f32[16,128]{1,0:T(8,128)S(1)} %bitcast.425, ...), kind=kLoop, calls=%fused_computation.127.clone.1 | loop fusion | flops 18348032 | bytes 245760 | tf_op jit(solution)/shard_map/while/body/reduce_sum | solution.py:105
  204.6 4.2 %multiply_reduce_fusion.38 = f32[16,128]{1,0:T(8,128)S(1)} fusion(f32[16,128]{1,0:T(8,128)S(1)} %bitcast.378, f32[16,128]{1,0:T(8,128)S(1)} %bitcast.421, f32[16,128]{1,0:T(8,128)S(1)} %bitcast.511, f32[16,128]{1,0:T(8,128)S(1)} %bitcast.426, f32[16,128]{1,0:T(8,128)S(1)} %bitcast.516, f32[16,128]{1,0:T(8,128)S(1)} %bitcast.438, ...), kind=kLoop, calls=%fused_computation.133.clone.1 | loop fusion | flops 12843008 | bytes 196608 | tf_op jit(solution)/shard_map/while/body/reduce_sum | solution.py:102
  208.8 4.2 %multiply_reduce_fusion.37 = f32[16,128]{1,0:T(8,128)S(1)} fusion(f32[16,128]{1,0:T(8,128)S(1)} %bitcast.379, f32[16,128]{1,0:T(8,128)S(1)} %bitcast.502, f32[16,128]{1,0:T(8,128)S(1)} %bitcast.506, f32[16,128]{1,0:T(8,128)S(1)} %bitcast.422, f32[16,128]{1,0:T(8,128)S(1)} %bitcast.512, f32[16,128]{1,0:T(8,128)S(1)} %bitcast.432, ...), kind=kLoop, calls=%fused_computation.132.clone.1 | loop fusion | flops 12843008 | bytes 196608 | tf_op jit(solution)/shard_map/while/body/reduce_sum | solution.py:102
  213.1 5.3 %multiply_reduce_fusion.36 = f32[16,128]{1,0:T(8,128)S(1)} fusion(f32[16,128]{1,0:T(8,128)S(1)} %broadcast_multiply_fusion.10, f32[16,128]{1,0:T(8,128)S(1)} %bitcast.503, f32[16,128]{1,0:T(8,128)S(1)} %bitcast.507, f32[16,128]{1,0:T(8,128)S(1)} %bitcast.423, f32[16,128]{1,0:T(8,128)S(1)} %bitcast.513, f32[16,128]{1,0:T(8,128)S(1)} %bitcast.427, ...), kind=kLoop, calls=%fused_computation.131.clone.1 | loop fusion | flops 18348032 | bytes 245760 | tf_op jit(solution)/shard_map/while/body/reduce_sum | solution.py:103
  234.1 5.0 %multiply_reduce_fusion.40 = f32[16,128]{1,0:T(8,128)S(1)} fusion(f32[16,128]{1,0:T(8,128)S(1)} %broadcast_multiply_fusion.11, f32[16,128]{1,0:T(8,128)S(1)} %bitcast.501, f32[16,128]{1,0:T(8,128)S(1)} %bitcast.505, f32[16,128]{1,0:T(8,128)S(1)} %bitcast.420, f32[16,128]{1,0:T(8,128)S(1)} %bitcast.510, f32[16,128]{1,0:T(8,128)S(1)} %bitcast.425, ...), kind=kLoop, calls=%fused_computation.127.clone.1 | loop fusion | flops 18348032 | bytes 245760 | tf_op jit(solution)/shard_map/while/body/reduce_sum | solution.py:105
  243.6 4.2 %multiply_reduce_fusion.38 = f32[16,128]{1,0:T(8,128)S(1)} fusion(f32[16,128]{1,0:T(8,128)S(1)} %bitcast.378, f32[16,128]{1,0:T(8,128)S(1)} %bitcast.421, f32[16,128]{1,0:T(8,128)S(1)} %bitcast.511, f32[16,128]{1,0:T(8,128)S(1)} %bitcast.426, f32[16,128]{1,0:T(8,128)S(1)} %bitcast.516, f32[16,128]{1,0:T(8,128)S(1)} %bitcast.438, ...), kind=kLoop, calls=%fused_computation.133.clone.1 | loop fusion | flops 12843008 | bytes 196608 | tf_op jit(solution)/shard_map/while/body/reduce_sum | solution.py:102
  247.8 4.2 %multiply_reduce_fusion.37 = f32[16,128]{1,0:T(8,128)S(1)} fusion(f32[16,128]{1,0:T(8,128)S(1)} %bitcast.379, f32[16,128]{1,0:T(8,128)S(1)} %bitcast.502, f32[16,128]{1,0:T(8,128)S(1)} %bitcast.506, f32[16,128]{1,0:T(8,128)S(1)} %bitcast.422, f32[16,128]{1,0:T(8,128)S(1)} %bitcast.512, f32[16,128]{1,0:T(8,128)S(1)} %bitcast.432, ...), kind=kLoop, calls=%fused_computation.132.clone.1 | loop fusion | flops 12843008 | bytes 196608 | tf_op jit(solution)/shard_map/while/body/reduce_sum | solution.py:102
  252.1 5.3 %multiply_reduce_fusion.36 = f32[16,128]{1,0:T(8,128)S(1)} fusion(f32[16,128]{1,0:T(8,128)S(1)} %broadcast_multiply_fusion.10, f32[16,128]{1,0:T(8,128)S(1)} %bitcast.503, f32[16,128]{1,0:T(8,128)S(1)} %bitcast.507, f32[16,128]{1,0:T(8,128)S(1)} %bitcast.423, f32[16,128]{1,0:T(8,128)S(1)} %bitcast.513, f32[16,128]{1,0:T(8,128)S(1)} %bitcast.427, ...), kind=kLoop, calls=%fused_computation.131.clone.1 | loop fusion | flops 18348032 | bytes 245760 | tf_op jit(solution)/shard_map/while/body/reduce_sum | solution.py:103
  (329 shorter events, 165.8 us)
Async XLA Ops:
  0.6 1.7 copy-start
  3.4 8.4 %copy-start.3 = (f32[6,8192]{1,0:T(8,128)S(1)}, f32[6,8192]{1,0:T(8,128)}, u32[]{:S(2)}) copy-start(f32[6,8192]{1,0:T(8,128)} %param.20) | copy-start | bytes 589828
  4.0 8.0 %collective-permute-start = (f32[1,16,8,128]{3,2,1,0:T(8,128)S(1)}, f32[1,16,8,128]{3,2,1,0:T(8,128)S(1)}, u32[]{:S(2)}, u32[]{:S(2)}) collective-permute-start(f32[1,16,8,128]{3,2,1,0:T(8,128)S(1)} %get-tuple-element.324), channel_id=1, source_target_pairs={{0,2},{2,4},{4,6},{6,8},{8,10},{10,12},{12,14},{14,16},{16,18},{18... | collective-permute-start | bytes 196616 | tf_op jit(solution)/shard_map/ppermute | solution.py:38
  7.7 6.5 %collective-permute-start.1 = (f32[1,16,8,128]{3,2,1,0:T(8,128)S(1)}, f32[1,16,8,128]{3,2,1,0:T(8,128)S(1)}, u32[]{:S(2)}, u32[]{:S(2)}) collective-permute-start(f32[1,16,8,128]{3,2,1,0:T(8,128)S(1)} %get-tuple-element.323), channel_id=1, source_target_pairs={{2,0},{4,2},{6,4},{8,6},{10,8},{12,10},{14,12},{16,14},{18,16},{20... | collective-permute-start | bytes 196616 | tf_op jit(solution)/shard_map/ppermute | solution.py:39
  10.3 0.7 copy-start.8
  14.8 4.5 %collective-permute-start.2 = (f32[1,16,8,128]{3,2,1,0:T(8,128)S(1)}, f32[1,16,8,128]{3,2,1,0:T(8,128)S(1)}, u32[]{:S(2)}, u32[]{:S(2)}) collective-permute-start(f32[1,16,8,128]{3,2,1,0:T(8,128)S(1)} %get-tuple-element.322), channel_id=1, source_target_pairs={{0,1},{2,3},{4,5},{6,7},{8,9},{10,11},{12,13},{14,15},{16,17},{18,... | collective-permute-start | bytes 196616 | tf_op jit(solution)/shard_map/ppermute | solution.py:38
  18.0 5.0 %collective-permute-start.3 = (f32[1,16,8,128]{3,2,1,0:T(8,128)S(1)}, f32[1,16,8,128]{3,2,1,0:T(8,128)S(1)}, u32[]{:S(2)}, u32[]{:S(2)}) collective-permute-start(f32[1,16,8,128]{3,2,1,0:T(8,128)S(1)} %get-tuple-element.321), channel_id=1, source_target_pairs={{1,0},{3,2},{5,4},{7,6},{9,8},{11,10},{13,12},{15,14},{17,16},{19,... | collective-permute-start | bytes 196616 | tf_op jit(solution)/shard_map/ppermute | solution.py:39
  62.5 3.2 %collective-permute-start.4 = (f32[1,16,9,128]{3,2,1,0:T(8,128)S(1)}, f32[1,16,9,128]{3,2,1,0:T(8,128)S(1)}, u32[]{:S(2)}, u32[]{:S(2)}) collective-permute-start(f32[1,16,9,128]{3,2,1,0:T(8,128)S(1)} %get-tuple-element.289), channel_id=1, source_target_pairs={{0,1},{2,3},{4,5},{6,7},{8,9},{10,11},{12,13},{14,15},{16,17},{18,... | collective-permute-start | bytes 221192 | tf_op jit(solution)/shard_map/ppermute | solution.py:38
  63.8 5.7 %collective-permute-start.5 = (f32[1,16,9,128]{3,2,1,0:T(8,128)S(1)}, f32[1,16,9,128]{3,2,1,0:T(8,128)S(1)}, u32[]{:S(2)}, u32[]{:S(2)}) collective-permute-start(f32[1,16,9,128]{3,2,1,0:T(8,128)S(1)} %get-tuple-element.288), channel_id=1, source_target_pairs={{1,0},{3,2},{5,4},{7,6},{9,8},{11,10},{13,12},{15,14},{17,16},{19,... | collective-permute-start | bytes 221192 | tf_op jit(solution)/shard_map/ppermute | solution.py:39
  70.7 4.4 %copy-start.9 = (s32[2,16]{1,0:T(2,128)S(1)}, s32[2,16]{1,0:T(2,128)}, u32[]{:S(2)}) copy-start(s32[2,16]{1,0:T(2,128)} %param.26) | copy-start | bytes 388
  70.7 4.4 %collective-permute-start.6 = (f32[1,16,9,128]{3,2,1,0:T(8,128)S(1)}, f32[1,16,9,128]{3,2,1,0:T(8,128)S(1)}, u32[]{:S(2)}, u32[]{:S(2)}) collective-permute-start(f32[1,16,9,128]{3,2,1,0:T(8,128)S(1)} %get-tuple-element.291), channel_id=1, source_target_pairs={{0,2},{2,4},{4,6},{6,8},{8,10},{10,12},{12,14},{14,16},{16,18},{18... | collective-permute-start | bytes 221192 | tf_op jit(solution)/shard_map/ppermute | solution.py:38
  72.6 7.2 %collective-permute-start.7 = (f32[1,16,9,128]{3,2,1,0:T(8,128)S(1)}, f32[1,16,9,128]{3,2,1,0:T(8,128)S(1)}, u32[]{:S(2)}, u32[]{:S(2)}) collective-permute-start(f32[1,16,9,128]{3,2,1,0:T(8,128)S(1)} %get-tuple-element.290), channel_id=1, source_target_pairs={{2,0},{4,2},{6,4},{8,6},{10,8},{12,10},{14,12},{16,14},{18,16},{20... | collective-permute-start | bytes 221192 | tf_op jit(solution)/shard_map/ppermute | solution.py:39
  81.4 0.8 copy-start.5
  81.4 0.8 copy-start.6
  82.2 0.8 copy-start.4
  83.0 0.9 copy-start.1
  85.1 4.4 %collective-permute-start.8 = (f32[1,16,15,128]{3,2,1,0:T(8,128)S(1)}, f32[1,16,15,128]{3,2,1,0:T(8,128)S(1)}, u32[]{:S(2)}, u32[]{:S(2)}) collective-permute-start(f32[1,16,15,128]{3,2,1,0:T(8,128)S(1)} %get-tuple-element.312), channel_id=1, source_target_pairs={{0,2},{2,4},{4,6},{6,8},{8,10},{10,12},{12,14},{14,16},{16,18},{18... | collective-permute-start | bytes 368648 | tf_op jit(solution)/shard_map/ppermute | solution.py:38
  87.0 7.2 %collective-permute-start.9 = (f32[1,16,15,128]{3,2,1,0:T(8,128)S(1)}, f32[1,16,15,128]{3,2,1,0:T(8,128)S(1)}, u32[]{:S(2)}, u32[]{:S(2)}) collective-permute-start(f32[1,16,15,128]{3,2,1,0:T(8,128)S(1)} %get-tuple-element.311), channel_id=1, source_target_pairs={{2,0},{4,2},{6,4},{8,6},{10,8},{12,10},{14,12},{16,14},{18,16},{20... | collective-permute-start | bytes 368648 | tf_op jit(solution)/shard_map/ppermute | solution.py:39
  94.9 4.3 %collective-permute-start.10 = (f32[1,16,15,128]{3,2,1,0:T(8,128)S(1)}, f32[1,16,15,128]{3,2,1,0:T(8,128)S(1)}, u32[]{:S(2)}, u32[]{:S(2)}) collective-permute-start(f32[1,16,15,128]{3,2,1,0:T(8,128)S(1)} %get-tuple-element.310), channel_id=1, source_target_pairs={{0,1},{2,3},{4,5},{6,7},{8,9},{10,11},{12,13},{14,15},{16,17},{18,... | collective-permute-start | bytes 368648 | tf_op jit(solution)/shard_map/ppermute | solution.py:38
  96.4 7.0 %collective-permute-start.11 = (f32[1,16,15,128]{3,2,1,0:T(8,128)S(1)}, f32[1,16,15,128]{3,2,1,0:T(8,128)S(1)}, u32[]{:S(2)}, u32[]{:S(2)}) collective-permute-start(f32[1,16,15,128]{3,2,1,0:T(8,128)S(1)} %get-tuple-element.309), channel_id=1, source_target_pairs={{1,0},{3,2},{5,4},{7,6},{9,8},{11,10},{13,12},{15,14},{17,16},{19,... | collective-permute-start | bytes 368648 | tf_op jit(solution)/shard_map/ppermute | solution.py:39
  259.7 2.6 collective-permute-start.12
  261.0 4.7 %collective-permute-start.13 = (f32[1,16,4,128]{3,2,1,0:T(4,128)S(1)}, f32[1,16,4,128]{3,2,1,0:T(4,128)S(1)}, u32[]{:S(2)}, u32[]{:S(2)}) collective-permute-start(f32[1,16,4,128]{3,2,1,0:T(4,128)S(1)} %get-tuple-element.307), channel_id=1, source_target_pairs={{1,0},{3,2},{5,4},{7,6},{9,8},{11,10},{13,12},{15,14},{17,16},{19,... | collective-permute-start | bytes 98312 | tf_op jit(solution)/shard_map/ppermute | solution.py:39
  266.8 5.4 %collective-permute-start.14 = (f32[1,16,4,128]{3,2,1,0:T(4,128)S(1)}, f32[1,16,4,128]{3,2,1,0:T(4,128)S(1)}, u32[]{:S(2)}, u32[]{:S(2)}) collective-permute-start(f32[1,16,4,128]{3,2,1,0:T(4,128)S(1)} %get-tuple-element.320), channel_id=1, source_target_pairs={{0,2},{2,4},{4,6},{6,8},{8,10},{10,12},{12,14},{14,16},{16,18},{18... | collective-permute-start | bytes 98312 | tf_op jit(solution)/shard_map/ppermute | solution.py:38
  268.7 6.1 %collective-permute-start.15 = (f32[1,16,4,128]{3,2,1,0:T(4,128)S(1)}, f32[1,16,4,128]{3,2,1,0:T(4,128)S(1)}, u32[]{:S(2)}, u32[]{:S(2)}) collective-permute-start(f32[1,16,4,128]{3,2,1,0:T(4,128)S(1)} %get-tuple-element.319), channel_id=1, source_target_pairs={{2,0},{4,2},{6,4},{8,6},{10,8},{12,10},{14,12},{16,14},{18,16},{20... | collective-permute-start | bytes 98312 | tf_op jit(solution)/shard_map/ppermute | solution.py:39
  (2 other events, 1.3 us)
where the time goes:
time: 281 us; the launch traced here: 277 us
  other arithmetic  195 us (69%)
  starting transfers between devices  31.1 us (11%)
  waiting for transfers between devices  26.8 us (10%)
  local copies, waits for them, and re-layouts  20.1 us (7%)
    reduce_sum x12, other arithmetic, force_terms(): jnp.sum(second_mass * pull_term, axis=2)  50.8 us
    reduce_sum x12, other arithmetic, force_terms(): jnp.sum(first_mass * pull_term, axis=1)  47.7 us
    ppermute x8, waiting for transfers between devices, extended(): after = lax.ppermute(first, axis, down)  24.8 us
    reduce_sum x4, other arithmetic, gradient_terms(): to_second.append(jnp.sum(product * first_volume, axis=1))  22.8 us
    reduce_sum x4, other arithmetic, force_terms(): to_first.append(jnp.sum(second_mass * heating, axis=2))  21.2 us
    reduce_sum x4, other arithmetic, force_terms(): to_second.append(jnp.sum(first_mass * heating, axis=1))  20.1 us
    ppermute x8, starting transfers between devices, extended(): before = lax.ppermute(last, axis, up)  16.7 us
    ppermute x8, starting transfers between devices, extended(): after = lax.ppermute(first, axis, down)  14.3 us
  transfers between devices with their start and end apart: 16, of which 10 were waited for; matrix products, arithmetic and copies ran while one was open for 2% of the time, Pallas kernels for 0%

commit v1 on v0

v1 whole, which is shorter than its diff:
```python
import functools
import math

import jax
import jax.numpy as jnp
from jax import lax
from jax.experimental import pallas as pl
from jax.experimental.pallas import tpu as pltpu
from jax.sharding import PartitionSpec as P

MESH = pl.DeviceIdType.MESH
F32 = jnp.float32
BF16 = jnp.bfloat16
SWEEPS = 3
UNROLL = 4
ROWS = 8
R1 = 5 * ROWS
R2 = 9 * ROWS


SMOOTHING = 1.0
KERNEL_SCALE = -105.0 / (16.0 * math.pi)
TIME_STEP = 0.05
SHEAR_MODULUS = 1.0
BULK_MODULUS = 2.0
DENSITY_REF = 1.0
YIELD_BASE = 0.3
HARDEN_COEF = 2.0
HARDEN_EXPONENT = 0.31
RATE_COEF = 0.025
RATE_REF = 0.02
THERMAL_EXPONENT = 1.09
ENERGY_REF = 1.0
VISCOUS_ALPHA = 1.0
VISCOUS_BETA = 2.0
SOFTENING = 0.01
STRESS_FLOOR = 0.1


def power(base, exponent):
    return jnp.exp(exponent * jnp.log(base))


def sym_matrix(components):
    return [
        [components[0], components[3], components[5]],
        [components[3], components[1], components[4]],
        [components[5], components[4], components[2]],
    ]


def update_material(velocity_grad, deviator, plastic, energy, density):
    gradient_rows = [[velocity_grad[3 * a + b] for b in range(3)] for a in range(3)]
    strain = [
        [0.5 * (gradient_rows[a][b] + gradient_rows[b][a]) for b in range(3)] for a in range(3)
    ]
    rotation = [
        [0.5 * (gradient_rows[a][b] - gradient_rows[b][a]) for b in range(3)] for a in range(3)
    ]
    trace_rate = strain[0][0] + strain[1][1] + strain[2][2]
    new_density = density * jnp.exp(-TIME_STEP * trace_rate)
    mean_normal = (deviator[0] + deviator[1] + deviator[2]) / 3.0
    previous = sym_matrix(
        [
            deviator[0] - mean_normal,
            deviator[1] - mean_normal,
            deviator[2] - mean_normal,
            deviator[3],
            deviator[4],
            deviator[5],
        ]
    )
    shear_rate = [
        [strain[a][b] - trace_rate / 3.0 if a == b else strain[a][b] for b in range(3)]
        for a in range(3)
    ]
    trial_stress = []
    for a in range(3):
        trial_row = []
        for b in range(3):
            rate_term = 2.0 * SHEAR_MODULUS * shear_rate[a][b]
            for k in range(3):
                rate_term = (
                    rate_term + rotation[a][k] * previous[k][b] - previous[a][k] * rotation[k][b]
                )
            trial_row.append(previous[a][b] + TIME_STEP * rate_term)
        trial_stress.append(trial_row)
    trial_parts = [
        trial_stress[0][0],
        trial_stress[1][1],
        trial_stress[2][2],
        trial_stress[0][1],
        trial_stress[1][2],
        trial_stress[2][0],
    ]
    contract = (
        trial_parts[0] * trial_parts[0]
        + trial_parts[1] * trial_parts[1]
        + trial_parts[2] * trial_parts[2]
        + 2.0
        * (
            trial_parts[3] * trial_parts[3]
            + trial_parts[4] * trial_parts[4]
            + trial_parts[5] * trial_parts[5]
        )
    )
    equivalent = jnp.sqrt(1.5 * contract)
    rate_square = shear_rate[0][0] * shear_rate[0][0]
    for a in range(3):
        for b in range(3):
            if a + b > 0:
                rate_square = rate_square + shear_rate[a][b] * shear_rate[a][b]
    rate_equiv = jnp.sqrt(2.0 / 3.0 * rate_square)
    rate_factor = 1.0 + RATE_COEF * jnp.log(jnp.maximum(rate_equiv / RATE_REF, 1.0))
    homologous = energy / (energy + ENERGY_REF)
    scale_now = rate_factor * (1.0 - power(homologous, THERMAL_EXPONENT))
    tangent = (
        3.0 * SHEAR_MODULUS
        + HARDEN_COEF * HARDEN_EXPONENT * power(plastic, HARDEN_EXPONENT - 1.0) * scale_now
    )
    increment = jnp.zeros_like(plastic)
    for sweep_index in range(SWEEPS):
        flow_stress = (
            YIELD_BASE + HARDEN_COEF * power(plastic + increment, HARDEN_EXPONENT)
        ) * scale_now
        increment = jnp.maximum(
            increment + (equivalent - 3.0 * SHEAR_MODULUS * increment - flow_stress) / tangent, 0.0
        )
    shrink = 1.0 - 3.0 * SHEAR_MODULUS * increment / jnp.maximum(equivalent, STRESS_FLOOR)
    new_deviator = [component * shrink for component in trial_parts]
    pressure = BULK_MODULUS * (new_density / DENSITY_REF - 1.0)
    inverse_sq = 1.0 / (new_density * new_density)
    scaled = [
        (new_deviator[k] - pressure) * inverse_sq if k < 3 else new_deviator[k] * inverse_sq
        for k in range(6)
    ]
    sound_speed = jnp.sqrt((BULK_MODULUS + 4.0 / 3.0 * SHEAR_MODULUS) / new_density)
    return (new_deviator, plastic + increment, new_density, scaled, sound_speed)


def split_two(value):
    high = value.astype(BF16)
    return (high, (value - high.astype(F32)).astype(BF16))


def split_three(value):
    one = value.astype(BF16).astype(F32)
    rest = value - one
    two = rest.astype(BF16).astype(F32)
    return (one, two, rest - two)


def dot(left, right, contract=(1, 0)):
    return lax.dot_general(
        left, right, (((contract[0],), (contract[1],)), ((), ())), preferred_element_type=F32
    )


def reciprocal(value):
    guess = pl.reciprocal(value, approx=True)
    return guess * (2.0 - value * guess)


def sum_groups(row, first_value, second_value):
    f, s = split_three(first_value), split_three(second_value)
    left = jnp.where(row < 6, 1.0, 0.0)
    right = left
    for k in range(3):
        left = jnp.where(row == k, f[k], left)
        right = jnp.where(row == 3 + k, s[k], right)
    return left, right


def xyz_dot(row, left, right):
    return jnp.sum(jnp.where(row < 3, left * right, 0.0), axis=0, keepdims=True)


def swap(row, tile):
    return jnp.where(row < 3, pltpu.roll(tile, 5, 0), pltpu.roll(tile, 3, 0))


def centred(row, tile, centre):
    moved = jnp.where(row < 6, tile - centre, 1.0)
    along = xyz_dot(row, moved, swap(row, moved))
    return jnp.where(row == 7, along, moved), along


def geometry(row, first, second, first_along, second_along):
    a1, a2, a3 = split_three(first)
    b1, b2, b3 = split_three(second)
    order = (b1, b2, b1, b2, b3, b1)
    near = jnp.where(row < 3, -2.0, 0.0)
    cross = jnp.where(row < 6, -1.0, 0.0)
    swapped = [swap(row, b) * cross for b in (b1, b2, b3)]
    swapped = (swapped[0], swapped[1], swapped[0], swapped[1], swapped[2], swapped[0])
    norm_left, norm_right = sum_groups(
        row, xyz_dot(row, first, first), xyz_dot(row, second, second)
    )
    along_left, along_right = sum_groups(row, first_along, second_along)
    zero = jnp.zeros_like(first)
    left = jnp.concatenate([a1, a1, a2, a2, a1, a3, norm_left, along_left], 0).astype(BF16)
    right_one = jnp.concatenate([b * near for b in order] + [norm_right, zero], 0)
    right_two = jnp.concatenate(list(swapped) + [zero, along_right], 0)
    right = jnp.concatenate([right_one, right_two], 1).astype(BF16)
    both = dot(left, right, (0, 0))
    width = first.shape[1]
    return both[:, :width], both[:, width:]


def weigh(columns, high, low, side):
    count = columns.shape[0]
    top, rest = split_two(columns)
    both = dot(jnp.concatenate([top, rest], 0), high, side)
    return both[:count] + both[count:] + dot(top, low, side)


def gradient_columns(tile, moved):
    volume = tile[7:8]
    base = moved * volume
    return jnp.concatenate([base] + [base * moved[3 + a : 4 + a] for a in range(3)], 0)


def force_columns(row, tile, moved, stress):
    mass = tile[6:7]
    base = moved * mass
    cols = sym_matrix([stress[1 + k : 2 + k] for k in range(6)])
    turned = jnp.zeros_like(moved)
    first_row = jnp.logical_or(row == 0, row == 3)
    second_row = jnp.logical_or(row == 1, row == 4)
    for b in range(3):
        column = jnp.where(first_row, cols[0][b], jnp.where(second_row, cols[1][b], cols[2][b]))
        turned = turned + column * jnp.where(row < 3, moved[b : b + 1], moved[3 + b : 4 + b])
    inner = jnp.zeros_like(mass)
    for a in range(3):
        inner = inner + moved[a : a + 1] * turned[3 + a : 4 + a]
    turned = jnp.where(row < 6, turned, inner)
    return jnp.concatenate(
        [base]
        + [base * moved[3 + a : 4 + a] for a in range(3)]
        + [stress * mass, turned * mass],
        0,
    )


def hot(ids, rows):
    where = lax.broadcasted_iota(jnp.int32, (rows, ids.shape[1]), 0)
    return jnp.where(where == ids, 1.0, 0.0).astype(BF16)


def place(one_hot, value):
    high, low = split_two(value)
    return dot(one_hot, high) + dot(one_hot, low)


class Exchange:
    def __init__(self, axis, size, stage, sends, lands, send_sem, recv_sem):
        self.me = lax.axis_index(axis)
        self.size = size
        self.lands = lands
        self.copies = [
            pltpu.make_async_remote_copy(
                src_ref=sends[d],
                dst_ref=lands[d],
                send_sem=send_sem.at[stage, d],
                recv_sem=recv_sem.at[stage, d],
                device_id={axis: self.me + (1, -1)[d]},
                device_id_type=MESH,
            )
            for d in range(2)
        ]

    def start(self):
        low, high = self.me > 0, self.me < self.size - 1
        pl.when(high)(self.copies[0].start)
        pl.when(low)(self.copies[1].start)

        @pl.when(jnp.logical_not(low))
        def _():
            self.lands[0][...] = jnp.zeros(self.lands[0].shape, F32)

        @pl.when(jnp.logical_not(high))
        def _():
            self.lands[1][...] = jnp.zeros(self.lands[1].shape, F32)

    def wait(self):
        low, high = self.me > 0, self.me < self.size - 1
        pl.when(low)(self.copies[0].wait_recv)
        pl.when(high)(self.copies[1].wait_recv)

    def finish(self):
        low, high = self.me > 0, self.me < self.size - 1
        pl.when(high)(self.copies[0].wait_send)
        pl.when(low)(self.copies[1].wait_send)


def step_kernel(
    sizes,
    pairs_ref,
    slab_ref,
    tile_ref,
    ids_ref,
    position,
    velocity,
    live_mass,
    density,
    deviator,
    plastic,
    energy,
    motion,
    material,
    own_rows,
    table,
    stress_table,
    outgoing,
    arrived,
    slots,
    sums,
    sums_arrived,
    pulls,
    pulls_arrived,
    near_high,
    near_low,
    closing_ref,
    send_sem,
    recv_sem,
):
    n_slab, n_tile, nb, gs, pairs = sizes
    blk = live_mass.shape[1]
    ext = nb + 2 * gs
    full = ext + 2 * gs
    axes = (("slab", n_slab), ("tile", n_tile))

    barrier = pltpu.get_barrier_semaphore()
    expected = 0
    for axis, size in axes:
        me = lax.axis_index(axis)
        for shift, there in ((1, me < size - 1), (-1, me > 0)):

            @pl.when(there)
            def _(axis=axis, me=me, shift=shift):
                pl.semaphore_signal(
                    barrier, inc=1, device_id={axis: me + shift}, device_id_type=MESH
                )

            expected = expected + there.astype(jnp.int32)

    def put(field, value):
        own_rows[pl.ds(field, nb, stride=ROWS), :] = value

    def put_own(ref):
        ref[:nb] = own_rows[...].reshape(nb, ROWS, blk)

    for k in range(3):
        put(k, position[k])
        put(3 + k, velocity[k])
    put(6, live_mass[...])
    put(7, live_mass[...] / density[...])

    def spread(ref, stage, before=None):
        for step, (axis, size) in enumerate(axes):
            ids = (slab_ref, tile_ref)[step]
            at = stage + step
            mine = 2 * (stage // 4) + step
            for d in range(2):
                for k in range(gs):
                    outgoing[mine, d, k] = ref[ids[1 - d, k]]
            if before is not None and step == 0:
                before()
            swapping = Exchange(
                axis,
                size,
                at,
                [outgoing.at[mine, d] for d in range(2)],
                [arrived.at[mine, d] for d in range(2)],
                send_sem,
                recv_sem,
            )
            swapping.start()
            swapping.wait()
            base = (nb, ext)[step]
            for d in range(2):
                ref[base + d * gs : base + (d + 1) * gs] = arrived[mine, d]
            swapping.finish()

    put_own(table)
    spread(table, 0, before=lambda: pl.semaphore_wait(barrier, expected))

    row = lax.broadcasted_iota(jnp.int32, (ROWS, blk), 0)

    def tiles(ref, p):
        return ref[pairs_ref[0, p]], ref[pairs_ref[1, p]]

    def moved_tiles(p):
        first, second = tiles(table, p)
        centre = jnp.mean(first, axis=1, keepdims=True)
        one, one_along = centred(row, first, centre)
        two, two_along = centred(row, second, centre)
        return first, second, one, two, one_along, two_along

    def keep(slot, width, value):
        slots[pl.ds(pl.multiple_of(slot * width, ROWS), width), :] = value

    def gradient_pair(p):
        first, second, one, two, one_along, two_along = moved_tiles(p)
        radius_sq, approach = geometry(row, one, two, one_along, two_along)
        radius_sq = jnp.maximum(radius_sq, 1e-30)
        spread_now = jnp.maximum(1.0 - 0.5 * (radius_sq * lax.rsqrt(radius_sq)), 0.0)
        high, low = split_two(spread_now * spread_now * spread_now)
        near_high[p] = high
        near_low[p] = low
        closing_ref[p] = jnp.minimum(approach, 0.0) * reciprocal(radius_sq + SOFTENING)
        to_first = weigh(gradient_columns(second, two), high, low, (1, 1))
        to_second = weigh(gradient_columns(first, one), high, low, (1, 0))
        keep(p, R1, jnp.concatenate([to_first, one], 0))
        keep(pairs + p, R1, jnp.concatenate([to_second, two], 0))

    def force_pair(p):
        first, second, one, two, one_along, two_along = moved_tiles(p)
        first_stress, second_stress = tiles(stress_table, p)
        sound_left, sound_right = sum_groups(row, first_stress[7:8], second_stress[7:8])
        rho_left, rho_right = sum_groups(row, first_stress[0:1], second_stress[0:1])
        zero = jnp.zeros_like(row, F32)
        right_one = jnp.concatenate([sound_right, zero], 0)
        right_two = jnp.concatenate([zero, rho_right], 0)
        totals = dot(
            jnp.concatenate([sound_left, rho_left], 0).astype(BF16),
            jnp.concatenate([right_one, right_two], 1).astype(BF16),
            (0, 0),
        )
        sound, rho = totals[:, :blk], totals[:, blk:]
        high, low = near_high[p], near_low[p]
        near = high.astype(F32) + low.astype(F32)
        closing = closing_ref[p]
        viscous = near * closing * (4.0 * closing - sound) * reciprocal(rho)
        drag_high, drag_low = split_two(viscous)
        from_second = force_columns(row, second, two, second_stress)
        from_first = force_columns(row, first, one, first_stress)
        keep(
            p,
            R2,
            jnp.concatenate(
                [
                    weigh(from_second, high, low, (1, 1)),
                    weigh(from_second[:ROWS], drag_high, drag_low, (1, 1)),
                    one,
                    first_stress,
                ],
                0,
            ),
        )
        keep(
            pairs + p,
            R2,
            jnp.concatenate(
                [
                    weigh(from_first, high, low, (1, 0)),
                    weigh(from_first[:ROWS], drag_high, drag_low, (1, 0)),
                    two,
                    second_stress,
                ],
                0,
            ),
        )

    def all_pairs(one_pair):
        def some(step, carry):
            for k in range(UNROLL):
                one_pair(step * UNROLL + k)
            return carry

        lax.fori_loop(0, pairs // UNROLL, some, 0)
        for p in range(pairs // UNROLL * UNROLL, pairs):
            one_pair(p)

    pair_hot = hot(ids_ref[0:1, : 2 * pairs], full)
    tile_hot = hot(ids_ref[1:2, : 2 * gs], ext)
    slab_hot = hot(ids_ref[2:3, : 2 * gs], nb)

    def give_back(ref, landing, stage):
        width = ref.shape[0]
        for step, (axis, size) in ((1, axes[1]), (0, axes[0])):
            base = (nb, ext)[step]
            one_hot = (slab_hot, tile_hot)[step]
            at = stage + 1 - step
            swapping = Exchange(
                axis,
                size,
                at,
                [ref.at[:, pl.ds(base + gs, gs), :], ref.at[:, pl.ds(base, gs), :]],
                [landing.at[step, d] for d in range(2)],
                send_sem,
                recv_sem,
            )
            swapping.start()
            swapping.wait()
            for c in range(width):
                come = jnp.concatenate([landing[step, 0, c], landing[step, 1, c]], 0)
                ref[c, :base, :] = ref[c, :base, :] + place(one_hot, come)
            swapping.finish()

    all_pairs(gradient_pair)

    def slot_rows(r, width):
        return slots[pl.ds(r, 2 * pairs, stride=width), :]

    for a in range(3):
        speed = slot_rows(4 * ROWS + 3 + a, R1)
        plain = slot_rows((a + 1) * ROWS + 6, R1) - speed * slot_rows(6, R1)
        for b in range(3):
            bent = slot_rows((a + 1) * ROWS + b, R1) - speed * slot_rows(b, R1)
            sums[3 * a + b] = place(pair_hot, slot_rows(4 * ROWS + b, R1) * plain - bent)
    give_back(sums, sums_arrived, 2)

    velocity_grad = [sums[c, :nb, :] * KERNEL_SCALE for c in range(9)]
    new_deviator, new_plastic, new_density, scaled, sound_speed = update_material(
        velocity_grad, [deviator[k] for k in range(6)], plastic[...], energy[...], density[...]
    )
    for k in range(6):
        material[k] = new_deviator[k]
        put(1 + k, scaled[k])
    material[6] = new_plastic
    material[7] = new_density
    put(0, new_density)
    put(7, sound_speed)
    put_own(stress_table)
    spread(stress_table, 4)

    all_pairs(force_pair)

    def get(r):
        return slot_rows(r, R2)

    place_of = [get(7 * ROWS + k) for k in range(3)]
    own = sym_matrix([get(8 * ROWS + 1 + k) for k in range(6)])
    other = sym_matrix([get(4 * ROWS + 1 + k) for k in range(6)])
    weight = get(6)
    drag = get(6 * ROWS + 6)
    heat = jnp.zeros_like(weight)
    bent = [place_of[b] * weight - get(b) for b in range(3)]
    for a in range(3):
        speed = get(7 * ROWS + 3 + a)
        carried = get(3 + a)
        pull = get(6 * ROWS + a) - place_of[a] * drag - get(5 * ROWS + a)
        inner = place_of[a] * (get(5 * ROWS + 3 + a) - get(6 * ROWS + 3 + a))
        for b in range(3):
            pull = pull + own[a][b] * bent[b] + other[a][b] * place_of[b]
            inner = inner + own[a][b] * (place_of[b] * carried - get((a + 1) * ROWS + b))
        heat = heat + speed * pull - inner
        pulls[a] = place(pair_hot, pull)
    heat = heat + get(5 * ROWS + 6) - get(6 * ROWS + 7)
    pulls[3] = place(pair_hot, heat)
    give_back(pulls, pulls_arrived, 6)
    for k in range(3):
        motion[k] = pulls[k, :nb, :] * KERNEL_SCALE
    motion[3] = pulls[3, :nb, :] * (-0.5 * KERNEL_SCALE)


def body(
    sizes,
    position,
    velocity,
    particle_mass,
    density,
    deviator,
    plastic,
    energy,
    block_fill,
    pair_blocks,
    pair_count,
    slab_send,
    tile_send,
):
    n_slab, n_tile = sizes
    nb = block_fill.shape[0]
    blk = position.shape[1] // nb
    gs = slab_send.shape[1]
    pairs = pair_blocks.shape[1]
    full = nb + 4 * gs
    alive = lax.broadcasted_iota(jnp.int32, (nb, blk), 1) < block_fill[:, None]
    live_mass = jnp.where(alive, particle_mass.reshape(nb, blk), 0.0)
    first, second = pair_blocks[0], pair_blocks[1]
    live = jnp.arange(pairs, dtype=jnp.int32) < pair_count[0]
    lane = max(2 * pairs, 2 * gs)

    def line(values):
        return jnp.pad(values, (0, lane - values.shape[0]), constant_values=-1)

    ids = jnp.stack(
        [
            line(
                jnp.concatenate(
                    [
                        jnp.where(live, first, -1),
                        jnp.where(live & (first != second), second, -1),
                    ]
                )
            ),
            line(tile_send.reshape(-1)),
            line(slab_send.reshape(-1)),
        ]
    )
    smem = pl.BlockSpec(memory_space=pltpu.SMEM)
    vmem = pl.BlockSpec(memory_space=pltpu.VMEM)
    motion, material = pl.pallas_call(
        functools.partial(step_kernel, (n_slab, n_tile, nb, gs, pairs)),
        out_shape=(
            jax.ShapeDtypeStruct((4, nb, blk), F32),
            jax.ShapeDtypeStruct((8, nb, blk), F32),
        ),
        in_specs=[smem] * 3 + [vmem] * 8,
        out_specs=(vmem, vmem),
        scratch_shapes=[
            pltpu.VMEM((nb * ROWS, blk), F32),
            pltpu.VMEM((full, ROWS, blk), F32),
            pltpu.VMEM((full, ROWS, blk), F32),
            pltpu.VMEM((4, 2, gs, ROWS, blk), F32),
            pltpu.VMEM((4, 2, gs, ROWS, blk), F32),
            pltpu.VMEM((2 * pairs * R2, blk), F32),
            pltpu.VMEM((9, full, blk), F32),
            pltpu.VMEM((2, 2, 9, gs, blk), F32),
            pltpu.VMEM((4, full, blk), F32),
            pltpu.VMEM((2, 2, 4, gs, blk), F32),
            pltpu.VMEM((pairs, blk, blk), BF16),
            pltpu.VMEM((pairs, blk, blk), BF16),
            pltpu.VMEM((pairs, blk, blk), F32),
            pltpu.SemaphoreType.DMA((8, 2)),
            pltpu.SemaphoreType.DMA((8, 2)),
        ],
        compiler_params=pltpu.CompilerParams(
            collective_id=0, has_side_effects=True, vmem_limit_bytes=40 * 1024 * 1024
        ),
    )(
        pair_blocks,
        slab_send,
        tile_send,
        ids,
        position.reshape(3, nb, blk),
        velocity.reshape(3, nb, blk),
        live_mass,
        density.reshape(nb, blk),
        deviator.reshape(6, nb, blk),
        plastic.reshape(nb, blk),
        energy.reshape(nb, blk),
    )
    return motion.reshape(4, nb * blk), material.reshape(8, nb * blk)


def solution(mesh):
    placed = (
        P(None, ("slab", "tile")),
        P(None, ("slab", "tile")),
        P(("slab", "tile")),
        P(("slab", "tile")),
        P(None, ("slab", "tile")),
        P(("slab", "tile")),
        P(("slab", "tile")),
        P(("slab", "tile")),
        P(None, ("slab", "tile")),
        P(("slab", "tile")),
        P(None, ("slab", "tile")),
        P(None, ("slab", "tile")),
    )
    return jax.shard_map(
        functools.partial(body, (mesh.shape["slab"], mesh.shape["tile"])),
        mesh=mesh,
        in_specs=placed,
        out_specs=(P(None, ("slab", "tile")), P(None, ("slab", "tile"))),
        check_vma=False,
    )
```

time: 281 us -> 73.7 us (0.26); the launches traced: 277 us -> 73.4 us
  other arithmetic: 195 us -> 0.92 us
  Pallas kernels: 0 us -> 64.9 us
  starting transfers between devices: 31.1 us -> 0 us
  waiting for transfers between devices: 26.8 us -> 0 us
  local copies, waits for them, and re-layouts: 20.1 us -> 6.16 us
    reduce_sum x36 -> x0, other arithmetic: 163 us -> none  [the longest x12 50.8 us: force_terms(): jnp.sum(second_mass * pull_term, axis=2)]
    pallas_call x0 -> x1, Pallas kernels: none -> 64.9 us  [body(): pl.pallas_call(functools.partial(step_kernel, (n_slab, n_tile, nb, gs, pa...]
    ppermute x16 -> x0, starting transfers between devices: 31.1 us -> none  [the longest x8 16.7 us: extended(): before = lax.ppermute(last, axis, up)]
    ppermute x16 -> x0, waiting for transfers between devices: 26.8 us -> none  [the longest x8 24.8 us: extended(): after = lax.ppermute(first, axis, down)]
    scatter-add x24 -> x0, other arithmetic: 26.6 us -> none  [the longest x8 8.86 us: one_group(): summed = summed.at[first_rows].add(to_first * weights[:, None, None])]
    gather x20 -> x0, local copies, waits for them, and re-layouts: 11.4 us -> none  [the longest x8 4.52 us: one_group(): table_blocks[second_rows]]
    unnamed x27 -> x21, local copies, waits for them, and re-layouts: 4.18 us -> 5.98 us
  transfers between devices with their start and end apart: 16 -> 0, of which waited for: 10 -> 0; matrix products, arithmetic and copies ran while one was open for 2% -> 0% of each run, Pallas kernels for 0% -> 0%
where the time goes in v1:
time: 73.7 us; the launch traced here: 73.4 us
  Pallas kernels  64.9 us (88%)
  local copies, waits for them, and re-layouts  6.16 us (8%)
  between operations  1.37 us (2%)
  other arithmetic  0.92 us (1%)
    pallas_call x1, Pallas kernels, body(): pl.pallas_call(functools.partial(step_kernel, (n_slab, n_tile, nb, gs, pa...  64.9 us
    unnamed x21, local copies, waits for them, and re-layouts  5.98 us

profile of v1, /device:TPU:11, one launch (start us, length us, event | category | flops | bytes accessed | tf_op | source)
XLA Modules:
  0.0 73.4 jit_solution(15619987500525740702)
XLA Ops:
  1.3 0.0 copy-start.4
  1.3 0.7 copy-done.4
  2.0 0.0 copy-start.5
  2.0 0.1 reshape.39
  2.0 0.6 copy-done.5
  2.6 0.1 reshape.38
  2.7 0.7 copy-done.3
  3.4 0.1 add_bitcast_fusion
  3.5 0.6 copy-done.8
  4.1 0.8 %bitcast_select_fusion.live_mass = f32[64,128]{1,0:T(8,128)S(1)} fusion(f32[8192]{0:T(1024)} %param.14, s32[64]{0:T(128)S(1)} %copy-done.8), kind=kLoop, calls=%fused_computation.5 | loop fusion | flops 16384 | bytes 65792 | tf_op jit(solution)/shard_map/jit(_where)/select_n | solution.py:580
  5.0 0.0 copy-start.6
  5.0 0.0 copy-start.7
  5.0 1.0 %copy.25 = f32[1,6,64,128]{3,2,1,0:T(8,128)S(1)} copy(f32[1,6,64,128]{3,1,2,0:T(8,128)} %bitcast.42) | data formatting | bytes 393216
  6.0 0.0 copy-done.6
  6.0 0.0 copy-done.7
  6.0 0.0 copy-start
  6.1 0.0 copy-start.1
  6.1 0.0 copy-start.2
  6.1 0.7 copy-done
  6.8 0.0 copy-done.1
  6.8 0.0 copy-done.2
  6.8 64.9 %shard_map.131 = (f32[4,64,128]{2,1,0:T(8,128)S(1)}, f32[8,64,128]{2,1,0:T(8,128)S(1)}) custom-call(s32[2,64]{1,0:T(2,128)S(1)} %copy-done.3, s32[2,16]{1,0:T(2,128)S(1)} %copy-done.4, s32[2,16]{1,0:T(2,128)S(1)} %copy-done.5, s32[3,128]{1,0:T(4,128)S(1)} %pad_add_fusion.ids_ref, f32[3,64,128]{2,1,0:T(8,128)S(1)} %get-tuple-element.11.position, ...), custom_call_target="tpu_custom_call" | custom-call | tf_op jit(solution)/shard_map/pallas_call | solution.py:604
  71.8 0.7 %copy.26 = f32[1,4,64,128]{3,1,2,0:T(4,128)} copy(f32[1,4,64,128]{3,2,1,0:T(8,128)S(1)} %bitcast.38) | data formatting | bytes 262144
  72.5 0.9 %copy.24 = f32[1,8,64,128]{3,1,2,0:T(8,128)} copy(f32[1,8,64,128]{3,2,1,0:T(8,128)S(1)} %bitcast.37) | data formatting | bytes 524288
  (6 shorter events, 0.0 us)
Async XLA Ops:
  1.3 0.7 copy-start.4
  2.0 0.7 copy-start.5
  2.7 0.7 copy-start.3
  3.5 0.7 copy-start.8
  5.0 1.1 %copy-start.6 = (f32[3,8192]{1,0:T(4,128)S(1)}, f32[3,8192]{1,0:T(4,128)}, u32[]{:S(2)}) copy-start(f32[3,8192]{1,0:T(4,128)} %param.13) | copy-start | bytes 294916
  5.0 1.1 %copy-start.7 = (f32[3,8192]{1,0:T(4,128)S(1)}, f32[3,8192]{1,0:T(4,128)}, u32[]{:S(2)}) copy-start(f32[3,8192]{1,0:T(4,128)} %param.12) | copy-start | bytes 294916
  6.0 0.8 %copy-start = (f32[8192]{0:T(1024)S(1)}, f32[8192]{0:T(1024)}, u32[]{:S(2)}) copy-start(f32[8192]{0:T(1024)} %param.15) | copy-start | bytes 98308
  6.1 0.8 %copy-start.1 = (f32[8192]{0:T(1024)S(1)}, f32[8192]{0:T(1024)}, u32[]{:S(2)}) copy-start(f32[8192]{0:T(1024)} %param.17) | copy-start | bytes 98308
  6.1 0.8 %copy-start.2 = (f32[8192]{0:T(1024)S(1)}, f32[8192]{0:T(1024)}, u32[]{:S(2)}) copy-start(f32[8192]{0:T(1024)} %param.18) | copy-start | bytes 98308

commit v2 on v1

--- a/solution.py
+++ b/solution.py
@@ -12,7 +12,7 @@
 F32 = jnp.float32
 BF16 = jnp.bfloat16
 SWEEPS = 3
-UNROLL = 4
+UNROLL = 32
 ROWS = 8
 R1 = 5 * ROWS
 R2 = 9 * ROWS
@@ -210,8 +210,11 @@
 def weigh(columns, high, low, side):
     count = columns.shape[0]
     top, rest = split_two(columns)
-    both = dot(jnp.concatenate([top, rest], 0), high, side)
-    return both[:count] + both[count:] + dot(top, low, side)
+    left = jnp.concatenate(
+        [jnp.concatenate([top, top], 1), jnp.concatenate([rest, jnp.zeros_like(rest)], 1)], 0
+    )
+    both = dot(left, jnp.concatenate([high, low], side[1]), side)
+    return both[:count] + both[count:]
 
 
 def gradient_columns(tile, moved):
@@ -406,13 +409,18 @@
         radius_sq = jnp.maximum(radius_sq, 1e-30)
         spread_now = jnp.maximum(1.0 - 0.5 * (radius_sq * lax.rsqrt(radius_sq)), 0.0)
         high, low = split_two(spread_now * spread_now * spread_now)
-        near_high[p] = high
-        near_low[p] = low
-        closing_ref[p] = jnp.minimum(approach, 0.0) * reciprocal(radius_sq + SOFTENING)
+        closing = jnp.minimum(approach, 0.0) * reciprocal(radius_sq + SOFTENING)
         to_first = weigh(gradient_columns(second, two), high, low, (1, 1))
         to_second = weigh(gradient_columns(first, one), high, low, (1, 0))
-        keep(p, R1, jnp.concatenate([to_first, one], 0))
-        keep(pairs + p, R1, jnp.concatenate([to_second, two], 0))
+
+        def store():
+            near_high[p] = high
+            near_low[p] = low
+            closing_ref[p] = closing
+            keep(p, R1, jnp.concatenate([to_first, one], 0))
+            keep(pairs + p, R1, jnp.concatenate([to_second, two], 0))
+
+        return store
 
     def force_pair(p):
         first, second, one, two, one_along, two_along = moved_tiles(p)
@@ -435,42 +443,31 @@
         drag_high, drag_low = split_two(viscous)
         from_second = force_columns(row, second, two, second_stress)
         from_first = force_columns(row, first, one, first_stress)
-        keep(
-            p,
-            R2,
-            jnp.concatenate(
-                [
-                    weigh(from_second, high, low, (1, 1)),
-                    weigh(from_second[:ROWS], drag_high, drag_low, (1, 1)),
-                    one,
-                    first_stress,
-                ],
-                0,
-            ),
-        )
-        keep(
-            pairs + p,
-            R2,
-            jnp.concatenate(
-                [
-                    weigh(from_first, high, low, (1, 0)),
-                    weigh(from_first[:ROWS], drag_high, drag_low, (1, 0)),
-                    two,
-                    second_stress,
-                ],
-                0,
-            ),
-        )
+        to_first = [
+            weigh(from_second, high, low, (1, 1)),
+            weigh(from_second[:ROWS], drag_high, drag_low, (1, 1)),
+        ]
+        to_second = [
+            weigh(from_first, high, low, (1, 0)),
+            weigh(from_first[:ROWS], drag_high, drag_low, (1, 0)),
+        ]
+
+        def store():
+            keep(p, R2, jnp.concatenate(to_first + [one, first_stress], 0))
+            keep(pairs + p, R2, jnp.concatenate(to_second + [two, second_stress], 0))
+
+        return store
 
     def all_pairs(one_pair):
         def some(step, carry):
-            for k in range(UNROLL):
-                one_pair(step * UNROLL + k)
+            stores = [one_pair(step * UNROLL + k) for k in range(UNROLL)]
+            for store in stores:
+                store()
             return carry
 
         lax.fori_loop(0, pairs // UNROLL, some, 0)
         for p in range(pairs // UNROLL * UNROLL, pairs):
-            one_pair(p)
+            one_pair(p)()
 
     pair_hot = hot(ids_ref[0:1, : 2 * pairs], full)
     tile_hot = hot(ids_ref[1:2, : 2 * gs], ext)

time: 73.7 us -> 65.8 us (0.89)
  Pallas kernels: 64.9 us -> 57 us
    pallas_call x1, Pallas kernels: 64.9 us -> 57 us  [body(): pl.pallas_call(functools.partial(step_kernel, (n_slab, n_tile, nb, gs, pa...]
where the time goes in v2:
time: 65.8 us; the launch traced here: 65.4 us
  Pallas kernels  57 us (87%)
  local copies, waits for them, and re-layouts  6.16 us (9%)
  between operations  1.37 us (2%)
  other arithmetic  0.92 us (1%)
    pallas_call x1, Pallas kernels, body(): pl.pallas_call(functools.partial(step_kernel, (n_slab, n_tile, nb, gs, pa...  57 us
    unnamed x21, local copies, waits for them, and re-layouts  5.98 us

profile of v2, /device:TPU:11, one launch (start us, length us, event | category | flops | bytes accessed | tf_op | source)
XLA Modules:
  0.0 65.4 jit_solution(1097199106284971557)
XLA Ops:
  1.3 0.0 copy-start.4
  1.3 0.7 %copy-done.4 = s32[2,16]{1,0:T(2,128)S(1)} copy-done((s32[2,16]{1,0:T(2,128)S(1)}, s32[2,16]{1,0:T(2,128)}, u32[]{:S(2)}) %copy-start.4) | copy-done | bytes 152
  2.0 0.0 copy-start.5
  2.0 0.1 reshape.39
  2.0 0.6 copy-done.5
  2.6 0.1 reshape.38
  2.7 0.7 %copy-done.3 = s32[2,64]{1,0:T(2,128)S(1)} copy-done((s32[2,64]{1,0:T(2,128)S(1)}, s32[2,64]{1,0:T(2,128)}, u32[]{:S(2)}) %copy-start.3) | copy-done | bytes 536
  3.4 0.1 add_bitcast_fusion
  3.5 0.6 copy-done.8
  4.1 0.8 %bitcast_select_fusion.live_mass = f32[64,128]{1,0:T(8,128)S(1)} fusion(f32[8192]{0:T(1024)} %param.14, s32[64]{0:T(128)S(1)} %copy-done.8), kind=kLoop, calls=%fused_computation.5 | loop fusion | flops 16384 | bytes 65792 | tf_op jit(solution)/shard_map/jit(_where)/select_n | solution.py:577
  5.0 0.0 copy-start.6
  5.0 0.0 copy-start.7
  5.0 1.0 %copy.25 = f32[1,6,64,128]{3,2,1,0:T(8,128)S(1)} copy(f32[1,6,64,128]{3,1,2,0:T(8,128)} %bitcast.42) | data formatting | bytes 393216
  6.0 0.0 copy-done.6
  6.0 0.0 copy-done.7
  6.0 0.0 copy-start
  6.1 0.0 copy-start.1
  6.1 0.0 copy-start.2
  6.1 0.7 %copy-done = f32[8192]{0:T(1024)S(1)} copy-done((f32[8192]{0:T(1024)S(1)}, f32[8192]{0:T(1024)}, u32[]{:S(2)}) %copy-start) | copy-done | bytes 32792
  6.8 0.0 copy-done.1
  6.8 0.0 copy-done.2
  6.8 57.0 %shard_map.131 = (f32[4,64,128]{2,1,0:T(8,128)S(1)}, f32[8,64,128]{2,1,0:T(8,128)S(1)}) custom-call(s32[2,64]{1,0:T(2,128)S(1)} %copy-done.3, s32[2,16]{1,0:T(2,128)S(1)} %copy-done.4, s32[2,16]{1,0:T(2,128)S(1)} %copy-done.5, s32[3,128]{1,0:T(4,128)S(1)} %pad_add_fusion.ids_ref, f32[3,64,128]{2,1,0:T(8,128)S(1)} %get-tuple-element.11.position, ...), custom_call_target="tpu_custom_call" | custom-call | tf_op jit(solution)/shard_map/pallas_call | solution.py:601
  63.8 0.7 %copy.26 = f32[1,4,64,128]{3,1,2,0:T(4,128)} copy(f32[1,4,64,128]{3,2,1,0:T(8,128)S(1)} %bitcast.38) | data formatting | bytes 262144
  64.6 0.9 %copy.24 = f32[1,8,64,128]{3,1,2,0:T(8,128)} copy(f32[1,8,64,128]{3,2,1,0:T(8,128)S(1)} %bitcast.37) | data formatting | bytes 524288
  (6 shorter events, 0.0 us)
Async XLA Ops:
  1.3 0.7 %copy-start.4 = (s32[2,16]{1,0:T(2,128)S(1)}, s32[2,16]{1,0:T(2,128)}, u32[]{:S(2)}) copy-start(s32[2,16]{1,0:T(2,128)} %slab_ref.1) | copy-start | bytes 388
  2.0 0.7 %copy-start.5 = (s32[2,16]{1,0:T(2,128)S(1)}, s32[2,16]{1,0:T(2,128)}, u32[]{:S(2)}) copy-start(s32[2,16]{1,0:T(2,128)} %tile_ref.1) | copy-start | bytes 388
  2.7 0.7 %copy-start.3 = (s32[2,64]{1,0:T(2,128)S(1)}, s32[2,64]{1,0:T(2,128)}, u32[]{:S(2)}) copy-start(s32[2,64]{1,0:T(2,128)} %pairs_ref.1) | copy-start | bytes 1540
  3.5 0.7 %copy-start.8 = (s32[64]{0:T(128)S(1)}, s32[64]{0:T(128)}, u32[]{:S(2)}) copy-start(s32[64]{0:T(128)} %param.19) | copy-start | bytes 772
  5.0 1.1 %copy-start.6 = (f32[3,8192]{1,0:T(4,128)S(1)}, f32[3,8192]{1,0:T(4,128)}, u32[]{:S(2)}) copy-start(f32[3,8192]{1,0:T(4,128)} %param.13) | copy-start | bytes 294916
  5.0 1.1 %copy-start.7 = (f32[3,8192]{1,0:T(4,128)S(1)}, f32[3,8192]{1,0:T(4,128)}, u32[]{:S(2)}) copy-start(f32[3,8192]{1,0:T(4,128)} %param.12) | copy-start | bytes 294916
  6.0 0.8 %copy-start = (f32[8192]{0:T(1024)S(1)}, f32[8192]{0:T(1024)}, u32[]{:S(2)}) copy-start(f32[8192]{0:T(1024)} %param.15) | copy-start | bytes 98308
  6.1 0.8 %copy-start.1 = (f32[8192]{0:T(1024)S(1)}, f32[8192]{0:T(1024)}, u32[]{:S(2)}) copy-start(f32[8192]{0:T(1024)} %param.17) | copy-start | bytes 98308
  6.1 0.8 %copy-start.2 = (f32[8192]{0:T(1024)S(1)}, f32[8192]{0:T(1024)}, u32[]{:S(2)}) copy-start(f32[8192]{0:T(1024)} %param.18) | copy-start | bytes 98308

commit v3 on v2

--- a/solution.py
+++ b/solution.py
@@ -473,8 +473,15 @@
     tile_hot = hot(ids_ref[1:2, : 2 * gs], ext)
     slab_hot = hot(ids_ref[2:3, : 2 * gs], nb)
 
-    def give_back(ref, landing, stage):
+    def add_arrived(ref, landing, step, one_hot, low, high):
+        for c in range(ref.shape[0]):
+            come = jnp.concatenate([landing[step, 0, c], landing[step, 1, c]], 0)
+            ref[c, low:high, :] = ref[c, low:high, :] + place(one_hot[low:high], come)
+
+    def give_back(ref, landing, stage, contributions):
         width = ref.shape[0]
+        for c in range(width):
+            ref[c, ext:, :] = place(pair_hot[ext:], contributions[c])
         for step, (axis, size) in ((1, axes[1]), (0, axes[0])):
             base = (nb, ext)[step]
             one_hot = (slab_hot, tile_hot)[step]
@@ -489,10 +496,13 @@
                 recv_sem,
             )
             swapping.start()
+            if step == 1:
+                for c in range(width):
+                    ref[c, :ext, :] = place(pair_hot[:ext], contributions[c])
+            else:
+                add_arrived(ref, landing, 1, tile_hot, 0, nb)
             swapping.wait()
-            for c in range(width):
-                come = jnp.concatenate([landing[step, 0, c], landing[step, 1, c]], 0)
-                ref[c, :base, :] = ref[c, :base, :] + place(one_hot, come)
+            add_arrived(ref, landing, step, one_hot, nb * step, base)
             swapping.finish()
 
     all_pairs(gradient_pair)
@@ -500,13 +510,14 @@
     def slot_rows(r, width):
         return slots[pl.ds(r, 2 * pairs, stride=width), :]
 
+    contributions = []
     for a in range(3):
         speed = slot_rows(4 * ROWS + 3 + a, R1)
         plain = slot_rows((a + 1) * ROWS + 6, R1) - speed * slot_rows(6, R1)
         for b in range(3):
             bent = slot_rows((a + 1) * ROWS + b, R1) - speed * slot_rows(b, R1)
-            sums[3 * a + b] = place(pair_hot, slot_rows(4 * ROWS + b, R1) * plain - bent)
-    give_back(sums, sums_arrived, 2)
+            contributions.append(slot_rows(4 * ROWS + b, R1) * plain - bent)
+    give_back(sums, sums_arrived, 2, contributions)
 
     velocity_grad = [sums[c, :nb, :] * KERNEL_SCALE for c in range(9)]
     new_deviator, new_plastic, new_density, scaled, sound_speed = update_material(
@@ -533,6 +544,7 @@
     weight = get(6)
     drag = get(6 * ROWS + 6)
     heat = jnp.zeros_like(weight)
+    contributions = []
     bent = [place_of[b] * weight - get(b) for b in range(3)]
     for a in range(3):
         speed = get(7 * ROWS + 3 + a)
@@ -543,10 +555,10 @@
             pull = pull + own[a][b] * bent[b] + other[a][b] * place_of[b]
             inner = inner + own[a][b] * (place_of[b] * carried - get((a + 1) * ROWS + b))
         heat = heat + speed * pull - inner
-        pulls[a] = place(pair_hot, pull)
+        contributions.append(pull)
     heat = heat + get(5 * ROWS + 6) - get(6 * ROWS + 7)
-    pulls[3] = place(pair_hot, heat)
-    give_back(pulls, pulls_arrived, 6)
+    contributions.append(heat)
+    give_back(pulls, pulls_arrived, 6, contributions)
     for k in range(3):
         motion[k] = pulls[k, :nb, :] * KERNEL_SCALE
     motion[3] = pulls[3, :nb, :] * (-0.5 * KERNEL_SCALE)

time: 65.8 us -> 65.4 us (level)
  no operation moved by 1% of the time
where the time goes in v3:
time: 65.4 us; the launch traced here: 65.1 us
  Pallas kernels  56.6 us (87%)
  local copies, waits for them, and re-layouts  6.16 us (9%)
  between operations  1.37 us (2%)
  other arithmetic  0.92 us (1%)
    pallas_call x1, Pallas kernels, body(): pl.pallas_call(functools.partial(step_kernel, (n_slab, n_tile, nb, gs, pa...  56.6 us
    unnamed x21, local copies, waits for them, and re-layouts  5.98 us

profile of v3, /device:TPU:11, one launch (start us, length us, event | category | flops | bytes accessed | tf_op | source)
XLA Modules:
  0.0 65.1 jit_solution(12538971057551686383)
XLA Ops:
  1.3 0.0 copy-start.4
  1.3 0.7 %copy-done.4 = s32[2,16]{1,0:T(2,128)S(1)} copy-done((s32[2,16]{1,0:T(2,128)S(1)}, s32[2,16]{1,0:T(2,128)}, u32[]{:S(2)}) %copy-start.4) | copy-done | bytes 152
  2.0 0.1 reshape.39
  2.0 0.6 copy-done.5
  2.6 0.1 reshape.38
  2.7 0.0 copy-start.3
  2.7 0.7 %copy-done.3 = s32[2,64]{1,0:T(2,128)S(1)} copy-done((s32[2,64]{1,0:T(2,128)S(1)}, s32[2,64]{1,0:T(2,128)}, u32[]{:S(2)}) %copy-start.3) | copy-done | bytes 536
  3.4 0.1 add_bitcast_fusion
  3.5 0.6 copy-done.8
  4.1 0.8 %bitcast_select_fusion.live_mass = f32[64,128]{1,0:T(8,128)S(1)} fusion(f32[8192]{0:T(1024)} %param.14, s32[64]{0:T(128)S(1)} %copy-done.8), kind=kLoop, calls=%fused_computation.5 | loop fusion | flops 16384 | bytes 65792 | tf_op jit(solution)/shard_map/jit(_where)/select_n | solution.py:589
  5.0 0.0 copy-start.6
  5.0 0.0 copy-start.7
  5.0 1.0 %copy.25 = f32[1,6,64,128]{3,2,1,0:T(8,128)S(1)} copy(f32[1,6,64,128]{3,1,2,0:T(8,128)} %bitcast.42) | data formatting | bytes 393216
  6.0 0.0 copy-done.6
  6.0 0.0 copy-done.7
  6.0 0.0 copy-start
  6.1 0.0 copy-start.1
  6.1 0.0 copy-start.2
  6.1 0.7 %copy-done = f32[8192]{0:T(1024)S(1)} copy-done((f32[8192]{0:T(1024)S(1)}, f32[8192]{0:T(1024)}, u32[]{:S(2)}) %copy-start) | copy-done | bytes 32792
  6.8 0.0 copy-done.1
  6.8 0.0 copy-done.2
  6.8 56.6 %shard_map.131 = (f32[4,64,128]{2,1,0:T(8,128)S(1)}, f32[8,64,128]{2,1,0:T(8,128)S(1)}) custom-call(s32[2,64]{1,0:T(2,128)S(1)} %copy-done.3, s32[2,16]{1,0:T(2,128)S(1)} %copy-done.4, s32[2,16]{1,0:T(2,128)S(1)} %copy-done.5, s32[3,128]{1,0:T(4,128)S(1)} %pad_add_fusion.ids_ref, f32[3,64,128]{2,1,0:T(8,128)S(1)} %get-tuple-element.11.position, ...), custom_call_target="tpu_custom_call" | custom-call | tf_op jit(solution)/shard_map/pallas_call | solution.py:613
  63.5 0.7 %copy.26 = f32[1,4,64,128]{3,1,2,0:T(4,128)} copy(f32[1,4,64,128]{3,2,1,0:T(8,128)S(1)} %bitcast.38) | data formatting | bytes 262144
  64.2 0.9 %copy.24 = f32[1,8,64,128]{3,1,2,0:T(8,128)} copy(f32[1,8,64,128]{3,2,1,0:T(8,128)S(1)} %bitcast.37) | data formatting | bytes 524288
  (6 shorter events, 0.0 us)
Async XLA Ops:
  1.3 0.7 %copy-start.4 = (s32[2,16]{1,0:T(2,128)S(1)}, s32[2,16]{1,0:T(2,128)}, u32[]{:S(2)}) copy-start(s32[2,16]{1,0:T(2,128)} %slab_ref.1) | copy-start | bytes 388
  2.0 0.7 %copy-start.5 = (s32[2,16]{1,0:T(2,128)S(1)}, s32[2,16]{1,0:T(2,128)}, u32[]{:S(2)}) copy-start(s32[2,16]{1,0:T(2,128)} %tile_ref.1) | copy-start | bytes 388
  2.7 0.7 %copy-start.3 = (s32[2,64]{1,0:T(2,128)S(1)}, s32[2,64]{1,0:T(2,128)}, u32[]{:S(2)}) copy-start(s32[2,64]{1,0:T(2,128)} %pairs_ref.1) | copy-start | bytes 1540
  3.5 0.7 %copy-start.8 = (s32[64]{0:T(128)S(1)}, s32[64]{0:T(128)}, u32[]{:S(2)}) copy-start(s32[64]{0:T(128)} %param.19) | copy-start | bytes 772
  5.0 1.1 %copy-start.6 = (f32[3,8192]{1,0:T(4,128)S(1)}, f32[3,8192]{1,0:T(4,128)}, u32[]{:S(2)}) copy-start(f32[3,8192]{1,0:T(4,128)} %param.13) | copy-start | bytes 294916
  5.0 1.1 %copy-start.7 = (f32[3,8192]{1,0:T(4,128)S(1)}, f32[3,8192]{1,0:T(4,128)}, u32[]{:S(2)}) copy-start(f32[3,8192]{1,0:T(4,128)} %param.12) | copy-start | bytes 294916
  6.0 0.8 %copy-start = (f32[8192]{0:T(1024)S(1)}, f32[8192]{0:T(1024)}, u32[]{:S(2)}) copy-start(f32[8192]{0:T(1024)} %param.15) | copy-start | bytes 98308
  6.1 0.8 %copy-start.1 = (f32[8192]{0:T(1024)S(1)}, f32[8192]{0:T(1024)}, u32[]{:S(2)}) copy-start(f32[8192]{0:T(1024)} %param.17) | copy-start | bytes 98308
  6.1 0.8 %copy-start.2 = (f32[8192]{0:T(1024)S(1)}, f32[8192]{0:T(1024)}, u32[]{:S(2)}) copy-start(f32[8192]{0:T(1024)} %param.18) | copy-start | bytes 98308

commit v4 on v3

--- a/solution.py
+++ b/solution.py
@@ -324,6 +324,7 @@
     near_high,
     near_low,
     closing_ref,
+    moved_ref,
     send_sem,
     recv_sem,
 ):
@@ -417,13 +418,16 @@
             near_high[p] = high
             near_low[p] = low
             closing_ref[p] = closing
+            moved_ref[0, p] = one
+            moved_ref[1, p] = two
             keep(p, R1, jnp.concatenate([to_first, one], 0))
             keep(pairs + p, R1, jnp.concatenate([to_second, two], 0))
 
         return store
 
     def force_pair(p):
-        first, second, one, two, one_along, two_along = moved_tiles(p)
+        first, second = tiles(table, p)
+        one, two = moved_ref[0, p], moved_ref[1, p]
         first_stress, second_stress = tiles(stress_table, p)
         sound_left, sound_right = sum_groups(row, first_stress[7:8], second_stress[7:8])
         rho_left, rho_right = sum_groups(row, first_stress[0:1], second_stress[0:1])
@@ -632,6 +636,7 @@
             pltpu.VMEM((pairs, blk, blk), BF16),
             pltpu.VMEM((pairs, blk, blk), BF16),
             pltpu.VMEM((pairs, blk, blk), F32),
+            pltpu.VMEM((2, pairs, ROWS, blk), F32),
             pltpu.SemaphoreType.DMA((8, 2)),
             pltpu.SemaphoreType.DMA((8, 2)),
         ],

time: 65.4 us -> 65.3 us (level)
  no operation moved by 1% of the time
where the time goes in v4:
time: 65.3 us; the launch traced here: 65 us
  Pallas kernels  56.5 us (87%)
  local copies, waits for them, and re-layouts  6.16 us (9%)
  between operations  1.37 us (2%)
  other arithmetic  0.92 us (1%)
    pallas_call x1, Pallas kernels, body(): pl.pallas_call(functools.partial(step_kernel, (n_slab, n_tile, nb, gs, pa...  56.5 us
    unnamed x21, local copies, waits for them, and re-layouts  5.98 us

profile of v4, /device:TPU:11, one launch (start us, length us, event | category | flops | bytes accessed | tf_op | source)
XLA Modules:
  0.0 65.0 jit_solution(7315416086676489533)
XLA Ops:
  1.3 0.0 copy-start.4
  1.3 0.7 %copy-done.4 = s32[2,16]{1,0:T(2,128)S(1)} copy-done((s32[2,16]{1,0:T(2,128)S(1)}, s32[2,16]{1,0:T(2,128)}, u32[]{:S(2)}) %copy-start.4) | copy-done | bytes 152
  2.0 0.0 copy-start.5
  2.0 0.1 reshape.39
  2.0 0.6 copy-done.5
  2.6 0.1 reshape.38
  2.7 0.7 %copy-done.3 = s32[2,64]{1,0:T(2,128)S(1)} copy-done((s32[2,64]{1,0:T(2,128)S(1)}, s32[2,64]{1,0:T(2,128)}, u32[]{:S(2)}) %copy-start.3) | copy-done | bytes 536
  3.4 0.1 add_bitcast_fusion
  3.5 0.6 copy-done.8
  4.1 0.8 %bitcast_select_fusion.live_mass = f32[64,128]{1,0:T(8,128)S(1)} fusion(f32[8192]{0:T(1024)} %param.14, s32[64]{0:T(128)S(1)} %copy-done.8), kind=kLoop, calls=%fused_computation.5 | loop fusion | flops 16384 | bytes 65792 | tf_op jit(solution)/shard_map/jit(_where)/select_n | solution.py:593
  5.0 0.0 copy-start.6
  5.0 0.0 copy-start.7
  5.0 1.0 %copy.25 = f32[1,6,64,128]{3,2,1,0:T(8,128)S(1)} copy(f32[1,6,64,128]{3,1,2,0:T(8,128)} %bitcast.42) | data formatting | bytes 393216
  6.0 0.0 copy-done.6
  6.0 0.0 copy-done.7
  6.0 0.0 copy-start
  6.1 0.0 copy-start.1
  6.1 0.0 copy-start.2
  6.1 0.7 %copy-done = f32[8192]{0:T(1024)S(1)} copy-done((f32[8192]{0:T(1024)S(1)}, f32[8192]{0:T(1024)}, u32[]{:S(2)}) %copy-start) | copy-done | bytes 32792
  6.8 0.0 copy-done.1
  6.8 0.0 copy-done.2
  6.8 56.5 %shard_map.131 = (f32[4,64,128]{2,1,0:T(8,128)S(1)}, f32[8,64,128]{2,1,0:T(8,128)S(1)}) custom-call(s32[2,64]{1,0:T(2,128)S(1)} %copy-done.3, s32[2,16]{1,0:T(2,128)S(1)} %copy-done.4, s32[2,16]{1,0:T(2,128)S(1)} %copy-done.5, s32[3,128]{1,0:T(4,128)S(1)} %pad_add_fusion.ids_ref, f32[3,64,128]{2,1,0:T(8,128)S(1)} %get-tuple-element.11.position, ...), custom_call_target="tpu_custom_call" | custom-call | tf_op jit(solution)/shard_map/pallas_call | solution.py:617
  63.4 0.7 %copy.26 = f32[1,4,64,128]{3,1,2,0:T(4,128)} copy(f32[1,4,64,128]{3,2,1,0:T(8,128)S(1)} %bitcast.38) | data formatting | bytes 262144
  64.1 0.9 %copy.24 = f32[1,8,64,128]{3,1,2,0:T(8,128)} copy(f32[1,8,64,128]{3,2,1,0:T(8,128)S(1)} %bitcast.37) | data formatting | bytes 524288
  (6 shorter events, 0.0 us)
Async XLA Ops:
  1.3 0.7 %copy-start.4 = (s32[2,16]{1,0:T(2,128)S(1)}, s32[2,16]{1,0:T(2,128)}, u32[]{:S(2)}) copy-start(s32[2,16]{1,0:T(2,128)} %slab_ref.1) | copy-start | bytes 388
  2.0 0.7 %copy-start.5 = (s32[2,16]{1,0:T(2,128)S(1)}, s32[2,16]{1,0:T(2,128)}, u32[]{:S(2)}) copy-start(s32[2,16]{1,0:T(2,128)} %tile_ref.1) | copy-start | bytes 388
  2.7 0.7 %copy-start.3 = (s32[2,64]{1,0:T(2,128)S(1)}, s32[2,64]{1,0:T(2,128)}, u32[]{:S(2)}) copy-start(s32[2,64]{1,0:T(2,128)} %pairs_ref.1) | copy-start | bytes 1540
  3.5 0.7 %copy-start.8 = (s32[64]{0:T(128)S(1)}, s32[64]{0:T(128)}, u32[]{:S(2)}) copy-start(s32[64]{0:T(128)} %param.19) | copy-start | bytes 772
  5.0 1.1 %copy-start.6 = (f32[3,8192]{1,0:T(4,128)S(1)}, f32[3,8192]{1,0:T(4,128)}, u32[]{:S(2)}) copy-start(f32[3,8192]{1,0:T(4,128)} %param.13) | copy-start | bytes 294916
  5.0 1.1 %copy-start.7 = (f32[3,8192]{1,0:T(4,128)S(1)}, f32[3,8192]{1,0:T(4,128)}, u32[]{:S(2)}) copy-start(f32[3,8192]{1,0:T(4,128)} %param.12) | copy-start | bytes 294916
  6.0 0.8 %copy-start = (f32[8192]{0:T(1024)S(1)}, f32[8192]{0:T(1024)}, u32[]{:S(2)}) copy-start(f32[8192]{0:T(1024)} %param.15) | copy-start | bytes 98308
  6.1 0.8 %copy-start.1 = (f32[8192]{0:T(1024)S(1)}, f32[8192]{0:T(1024)}, u32[]{:S(2)}) copy-start(f32[8192]{0:T(1024)} %param.17) | copy-start | bytes 98308
  6.1 0.8 %copy-start.2 = (f32[8192]{0:T(1024)S(1)}, f32[8192]{0:T(1024)}, u32[]{:S(2)}) copy-start(f32[8192]{0:T(1024)} %param.18) | copy-start | bytes 98308
